TPU v7x, 256 devices: a whole 4x4x8 slice. The times are simulated.
256 devices in a mesh: gx: 16 (over z, x_hi), gy: 4 (over y), gz: 4 (over x_lo, core).
Axes of the slice: x: 4 (x_hi: 2, x_lo: 2; x = x_hi * 2 + x_lo), y: 4, z: 8, core: 2. Of those that a mesh axis runs over, the one named last changes fastest.
Arguments:
- populations: float32 [19, 128, 32, 512], P(None, 'gx', 'gy', 'gz'), may hold values from 0.005 to 0.6, as said below
- design: float32 [128, 32, 512], P('gx', 'gy', 'gz'), may hold values from 0 to 1
- flags: int32 [128, 32, 512], P('gx', 'gy', 'gz'), may hold values from 0 to 3
- adjoint_seed: float32 [19, 128, 32, 512], P(None, 'gx', 'gy', 'gz'), may hold values from -120 to 120
Outputs:
- design_grad: float32 [128, 32, 512], P('gx', 'gy', 'gz')
- grad_rms: float32 [], replicated
Inputs may be any that keep to these rules, and one draw needn't show every extreme that they name: `populations`: every population is positive.
All inputs are finite; a program needn't handle non-finite values.
Results may differ from a plain program's by a relative error of at most 0.0003.
Values sent between devices are 32-bit elements; how exact they have to be, the bound alone decides.
A program may use at most 64 MiB of HBM per device.

v0:
```python
import jax
import jax.numpy as jnp
from jax import lax
from jax.sharding import PartitionSpec as P

STEPS = 2


lattice_velocities = [
    (0, 0, 0),
    (1, 0, 0),
    (-1, 0, 0),
    (0, 1, 0),
    (0, -1, 0),
    (0, 0, 1),
    (0, 0, -1),
    (1, 1, 0),
    (-1, -1, 0),
    (1, -1, 0),
    (-1, 1, 0),
    (1, 0, 1),
    (-1, 0, -1),
    (1, 0, -1),
    (-1, 0, 1),
    (0, 1, 1),
    (0, -1, -1),
    (0, 1, -1),
    (0, -1, 1),
]
opposite_index = [0, 2, 1, 4, 3, 6, 5, 8, 7, 10, 9, 12, 11, 14, 13, 16, 15, 18, 17]
lattice_weights = [1.0 / 3.0] + [1.0 / 18.0] * 6 + [1.0 / 36.0] * 12
hat_weights = [1.0, 2.0, 3.0, 4.0, 5.0, 4.0, 3.0, 2.0, 1.0]
relax_rate = 1.6
kappa_top = 0.5
inlet_speed = 0.05
norm_eps = 1e-06


def with_halo(cells, sides, width, closed):
    for axis, dim in sides:
        count = lax.axis_size(axis)
        ends = count if closed else count - 1
        head = lax.slice_in_dim(cells, 0, width, axis=dim)
        tail = lax.slice_in_dim(cells, cells.shape[dim] - width, cells.shape[dim], axis=dim)
        cells = jnp.concatenate(
            [
                lax.ppermute(tail, axis, [(i, (i + 1) % count) for i in range(ends)]),
                cells,
                lax.ppermute(head, axis, [((i + 1) % count, i) for i in range(ends)]),
            ],
            axis=dim,
        )
    return cells


def equilibrium(density, speed_x, speed_y, speed_z):
    square = speed_x * speed_x + speed_y * speed_y + speed_z * speed_z
    layers = []
    for direction in range(19):
        projected = 0.0
        for component, speed_value in zip(
            lattice_velocities[direction], (speed_x, speed_y, speed_z)
        ):
            if component != 0:
                projected = projected + component * speed_value
        layers.append(
            lattice_weights[direction]
            * density
            * (1.0 + 3.0 * projected + 4.5 * projected * projected - 1.5 * square)
        )
    return layers


def moment(state, dimension):
    total = 0.0
    for direction in range(19):
        component = lattice_velocities[direction][dimension]
        if component != 0:
            total = total + component * state[direction]
    return total


def collide(state, kappa, flags):
    density = jnp.sum(state, axis=0)
    speed_x = moment(state, 0) / density
    speed_y = moment(state, 1) / density
    speed_z = moment(state, 2) / density
    balance = jnp.stack(equilibrium(density, speed_x, speed_y, speed_z))
    relax = jnp.where(flags == 3, 1.0, relax_rate).astype(state.dtype)
    relaxed = state - relax * (state - balance)
    flipped = jnp.stack([relaxed[other] for other in opposite_index])
    porous = (1.0 - kappa) * relaxed + kappa * flipped
    bounced = jnp.stack([state[other] for other in opposite_index])
    inflow = jnp.asarray(equilibrium(1.0, inlet_speed, 0.0, 0.0), dtype=state.dtype).reshape(
        19, 1, 1, 1
    )
    return jnp.where(flags == 1, bounced, jnp.where(flags == 2, inflow, porous))


def stream(state, heading):
    padded = with_halo(state, (("gx", 1), ("gy", 2), ("gz", 3)), 1, True)
    first, second, third = state.shape[1:]
    layers = []
    for direction in range(19):
        move_x, move_y, move_z = [
            heading * component for component in lattice_velocities[direction]
        ]
        layers.append(
            padded[
                direction,
                1 - move_x : 1 - move_x + first,
                1 - move_y : 1 - move_y + second,
                1 - move_z : 1 - move_z + third,
            ]
        )
    return jnp.stack(layers)


def sweep(padded, dimension):
    length = padded.shape[dimension] - 8
    total = 0.0
    for offset in range(9):
        total = total + hat_weights[offset] * lax.slice_in_dim(
            padded, offset, offset + length, axis=dimension
        )
    return total


def smooth(field):
    result = with_halo(field, (("gx", 0), ("gy", 1), ("gz", 2)), 4, False)
    for dimension in range(3):
        result = sweep(result, dimension)
    return result


def weight_sums(count, start, whole):
    positions = start + jnp.arange(count, dtype=jnp.int32)
    total = jnp.zeros((count,), jnp.float32)
    for offset in range(9):
        moved = positions + (offset - 4)
        inside = jnp.logical_and(moved >= 0, moved < whole)
        total = total + hat_weights[offset] * inside.astype(jnp.float32)
    return total


def body(populations, design, flags, adjoint_seed):
    width_first, width_second, width_third = design.shape
    count_first = lax.axis_size("gx")
    count_second = lax.axis_size("gy")
    count_third = lax.axis_size("gz")
    totals = (
        weight_sums(width_first, lax.axis_index("gx") * width_first, width_first * count_first)[
            :, None, None
        ]
        * weight_sums(
            width_second, lax.axis_index("gy") * width_second, width_second * count_second
        )[None, :, None]
        * weight_sums(width_third, lax.axis_index("gz") * width_third, width_third * count_third)[
            None, None, :
        ]
    )
    filtered = smooth(design) / totals
    kappa = kappa_top * (1.0 - filtered)
    states = [populations]
    current = populations
    number = 0
    current = stream(collide(current, kappa, flags), 1)
    states.append(current)
    adjoint = adjoint_seed
    kappa_grad = jnp.zeros_like(design)
    for number in reversed(range(STEPS)):
        pulled = stream(adjoint, -1)
        unused, pullback = jax.vjp(
            lambda state, porosity: collide(state, porosity, flags), states[number], kappa
        )
        adjoint, kappa_part = pullback(pulled)
        kappa_grad = kappa_grad + kappa_part
    raw_grad = smooth(-kappa_top * kappa_grad / totals)
    squares = lax.psum(jnp.sum(raw_grad * raw_grad), ("gx", "gy", "gz"))
    cells = width_first * width_second * width_third * count_first * count_second * count_third
    mean_square = squares / cells
    design_grad = raw_grad * lax.rsqrt(mean_square + norm_eps)
    return (design_grad, jnp.sqrt(mean_square))


def solution(mesh):
    return jax.shard_map(
        body,
        mesh=mesh,
        in_specs=(
            P(None, "gx", "gy", "gz"),
            P("gx", "gy", "gz"),
            P("gx", "gy", "gz"),
            P(None, "gx", "gy", "gz"),
        ),
        out_specs=(P("gx", "gy", "gz"), P()),
        check_vma=False,
    )
```

profile of v0, /device:TPU:1, one launch (start us, length us, event | category | flops | bytes accessed | tf_op | source)
XLA Modules:
  0.0 266.5 jit_solution(12154406623156871028)
XLA Ops:
  1.6 3.7 %collective-permute-start.1 = (f32[19,1,8,128]{3,2,1,0:T(8,128)S(1)}, f32[19,1,8,128]{3,2,1,0:T(8,128)S(1)}, u32[]{:S(2)}, u32[]{:S(2)}) collective-permute-start(f32[19,1,8,128]{3,2,1,0:T(8,128)S(1)} %get-tuple-element.105), channel_id=1, source_target_pairs={{0,16},{16,32},{32,48},{48,64},{64,80},{80,96},{96,112},{112,128},... | collective-permute-start | bytes 233480 | tf_op jit(solution)/shard_map/ppermute | solution.py:47
  5.3 5.4 %collective-permute-start = (f32[19,1,8,128]{3,2,1,0:T(8,128)S(1)}, f32[19,1,8,128]{3,2,1,0:T(8,128)S(1)}, u32[]{:S(2)}, u32[]{:S(2)}) collective-permute-start(f32[19,1,8,128]{3,2,1,0:T(8,128)S(1)} %get-tuple-element.106), channel_id=1, source_target_pairs={{16,0},{32,16},{48,32},{64,48},{80,64},{96,80},{112,96},{128,112},... | collective-permute-start | bytes 233480 | tf_op jit(solution)/shard_map/ppermute | solution.py:49
  20.2 3.2 %collective-permute-start.8 = (f32[16,4,128]{2,1,0:T(4,128)S(1)}, f32[16,4,128]{2,1,0:T(4,128)S(1)}, u32[]{:S(2)}, u32[]{:S(2)}) collective-permute-start(f32[16,4,128]{2,1,0:T(4,128)S(1)} %get-tuple-element.116), channel_id=1, source_target_pairs={{0,4},{4,8},{8,12},{1,5},{5,9},{9,13},{2,6},{6,10},{10,14},{3,7},{... | collective-permute-start | bytes 98312 | tf_op jit(solution)/shard_map/ppermute | solution.py:47
  24.8 3.3 %collective-permute-done.9 = f32[16,4,128]{2,1,0:T(4,128)S(1)} collective-permute-done((f32[16,4,128]{2,1,0:T(4,128)S(1)}, f32[16,4,128]{2,1,0:T(4,128)S(1)}, u32[]{:S(2)}, u32[]{:S(2)}) %collective-permute-start.9) | collective-permute-done | bytes 32800 | tf_op jit(solution)/shard_map/ppermute | solution.py:49
  28.2 4.5 %collective-permute-start.10 = (f32[16,16,4]{2,1,0:T(8,128)S(1)}, f32[16,16,4]{2,1,0:T(8,128)S(1)}, u32[]{:S(2)}, u32[]{:S(2)}) collective-permute-start(f32[16,16,4]{2,1,0:T(8,128)S(1)} %get-tuple-element.111), channel_id=1, source_target_pairs={{0,1},{1,2},{2,3},{4,5},{5,6},{6,7},{8,9},{9,10},{10,11},{12,13},{... | collective-permute-start | bytes 12296 | tf_op jit(solution)/shard_map/ppermute | solution.py:47
  32.7 1.9 collective-permute-start.11
  34.7 4.3 %collective-permute-done.11 = f32[16,16,4]{2,1,0:T(8,128)S(1)} collective-permute-done((f32[16,16,4]{2,1,0:T(8,128)S(1)}, f32[16,16,4]{2,1,0:T(8,128)S(1)}, u32[]{:S(2)}, u32[]{:S(2)}) %collective-permute-start.11) | collective-permute-done | bytes 4128 | tf_op jit(solution)/shard_map/ppermute | solution.py:49
  43.4 2.0 collective-permute-done.3
  47.4 2.1 copy.85
  50.4 1.8 collective-permute-start.5
  55.3 2.6 copy.88
  70.1 4.7 %collective-permute-start.12 = (f32[19,1,8,128]{3,2,1,0:T(8,128)S(1)}, f32[19,1,8,128]{3,2,1,0:T(8,128)S(1)}, u32[]{:S(2)}, u32[]{:S(2)}) collective-permute-start(f32[19,1,8,128]{3,2,1,0:T(8,128)S(1)} %get-tuple-element.85), channel_id=1, source_target_pairs={{0,16},{16,32},{32,48},{48,64},{64,80},{80,96},{96,112},{112,128},... | collective-permute-start | bytes 233480 | tf_op jit(solution)/shard_map/ppermute | solution.py:47
  74.9 4.1 %collective-permute-start.13 = (f32[19,1,8,128]{3,2,1,0:T(8,128)S(1)}, f32[19,1,8,128]{3,2,1,0:T(8,128)S(1)}, u32[]{:S(2)}, u32[]{:S(2)}) collective-permute-start(f32[19,1,8,128]{3,2,1,0:T(8,128)S(1)} %get-tuple-element.86), channel_id=1, source_target_pairs={{16,0},{32,16},{48,32},{64,48},{80,64},{96,80},{112,96},{128,112},... | collective-permute-start | bytes 233480 | tf_op jit(solution)/shard_map/ppermute | solution.py:49
  82.1 2.7 collective-permute-start.15
  88.9 1.7 fusion.403
  90.6 2.7 %copy.89 = f32[19,10,10,1]{0,3,2,1:T(1,128)} copy(f32[19,10,10,1]{3,2,1,0:T(8,128)} %get-tuple-element.54) | data formatting | bytes 15200 | tf_op jit(solution)/shard_map/slice | solution.py:44
  96.6 2.4 copy.90
  99.1 3.5 %copy.92 = f32[19,10,10,1]{3,2,1,0:T(8,128)} copy(f32[19,10,10,1]{0,3,2,1:T(1,128)} %collective-permute-done.17) | data formatting | bytes 15200 | tf_op jit(solution)/shard_map/ppermute | solution.py:49
  102.5 1.9 fusion.275
  107.0 5.7 %collective-permute-start.18 = (f32[19,1,8,128]{3,2,1,0:T(8,128)S(1)}, f32[19,1,8,128]{3,2,1,0:T(8,128)S(1)}, u32[]{:S(2)}, u32[]{:S(2)}) collective-permute-start(f32[19,1,8,128]{3,2,1,0:T(8,128)S(1)} %get-tuple-element.66), channel_id=1, source_target_pairs={{16,0},{32,16},{48,32},{64,48},{80,64},{96,80},{112,96},{128,112},... | collective-permute-start | bytes 233480 | tf_op jit(solution)/shard_map/ppermute | solution.py:49
  114.3 5.2 %collective-permute-done.19 = f32[19,1,8,128]{3,2,1,0:T(8,128)S(1)} collective-permute-done((f32[19,1,8,128]{3,2,1,0:T(8,128)S(1)}, f32[19,1,8,128]{3,2,1,0:T(8,128)S(1)}, u32[]{:S(2)}, u32[]{:S(2)}) %collective-permute-start.19) | collective-permute-done | bytes 77856 | tf_op jit(solution)/shard_map/ppermute | solution.py:47
  119.7 2.7 %collective-permute-start.20 = (f32[19,10,1,128]{3,2,1,0:T(1,128)S(1)}, f32[19,10,1,128]{3,2,1,0:T(1,128)S(1)}, u32[]{:S(2)}, u32[]{:S(2)}) collective-permute-start(f32[19,10,1,128]{3,2,1,0:T(1,128)S(1)} %get-tuple-element.58), channel_id=1, source_target_pairs={{4,0},{8,4},{12,8},{0,12},{5,1},{9,5},{13,9},{1,13},{6,2},{10,6},{... | collective-permute-start | bytes 291848 | tf_op jit(solution)/shard_map/ppermute | solution.py:49
  124.1 3.0 %collective-permute-done.21 = f32[19,10,1,128]{3,2,1,0:T(1,128)S(1)} collective-permute-done((f32[19,10,1,128]{3,2,1,0:T(1,128)S(1)}, f32[19,10,1,128]{3,2,1,0:T(1,128)S(1)}, u32[]{:S(2)}, u32[]{:S(2)}) %collective-permute-start.21) | collective-permute-done | bytes 97312 | tf_op jit(solution)/shard_map/ppermute | solution.py:47
  129.1 2.1 copy.93
  131.3 2.7 collective-permute-start.22
  137.9 2.7 %copy.96 = f32[19,10,10,1]{3,2,1,0:T(8,128)} copy(f32[19,10,10,1]{0,3,2,1:T(1,128)S(1)} %collective-permute-done.23) | data formatting | bytes 15200 | tf_op jit(solution)/shard_map/ppermute | solution.py:47
  155.9 4.7 %collective-permute-done.25 = f32[4,8,128]{2,1,0:T(8,128)S(1)} collective-permute-done((f32[4,8,128]{2,1,0:T(8,128)S(1)}, f32[4,8,128]{2,1,0:T(8,128)S(1)}, u32[]{:S(2)}, u32[]{:S(2)}) %collective-permute-start.25) | collective-permute-done | bytes 16416 | tf_op jit(solution)/shard_map/ppermute | solution.py:49
  163.3 3.3 %collective-permute-done.27 = f32[16,4,128]{2,1,0:T(4,128)S(1)} collective-permute-done((f32[16,4,128]{2,1,0:T(4,128)S(1)}, f32[16,4,128]{2,1,0:T(4,128)S(1)}, u32[]{:S(2)}, u32[]{:S(2)}) %collective-permute-start.27) | collective-permute-done | bytes 32800 | tf_op jit(solution)/shard_map/ppermute | solution.py:49
  166.7 4.9 %collective-permute-start.28 = (f32[16,16,4]{2,1,0:T(8,128)S(1)}, f32[16,16,4]{2,1,0:T(8,128)S(1)}, u32[]{:S(2)}, u32[]{:S(2)}) collective-permute-start(f32[16,16,4]{2,1,0:T(8,128)S(1)} %get-tuple-element.107), channel_id=1, source_target_pairs={{0,1},{1,2},{2,3},{4,5},{5,6},{6,7},{8,9},{9,10},{10,11},{12,13},{... | collective-permute-start | bytes 12296 | tf_op jit(solution)/shard_map/ppermute | solution.py:47
  171.6 1.9 collective-permute-start.29
  173.6 4.3 %collective-permute-done.29 = f32[16,16,4]{2,1,0:T(8,128)S(1)} collective-permute-done((f32[16,16,4]{2,1,0:T(8,128)S(1)}, f32[16,16,4]{2,1,0:T(8,128)S(1)}, u32[]{:S(2)}, u32[]{:S(2)}) %collective-permute-start.29) | collective-permute-done | bytes 4128 | tf_op jit(solution)/shard_map/ppermute | solution.py:49
  179.1 85.0 %psum.7 = f32[]{:T(128)} all-reduce(f32[]{:T(128)} %get-tuple-element.8), channel_id=1, replica_groups=mesh['gx'=16,'gy'=4,'gz'=4] {'gx','gy','gz'}, use_global_device_ids=true, to_apply=%region_6.7 | all-reduce | flops 1 | bytes 8 | tf_op jit(solution)/shard_map/psum | solution.py:179
  (337 shorter events, 75.4 us)
Async XLA Ops:
  1.6 37.9 %collective-permute-start.1 = (f32[19,1,8,128]{3,2,1,0:T(8,128)S(1)}, f32[19,1,8,128]{3,2,1,0:T(8,128)S(1)}, u32[]{:S(2)}, u32[]{:S(2)}) collective-permute-start(f32[19,1,8,128]{3,2,1,0:T(8,128)S(1)} %get-tuple-element.105), channel_id=1, source_target_pairs={{0,16},{16,32},{32,48},{48,64},{64,80},{80,96},{96,112},{112,128},... | collective-permute-start | bytes 233480 | tf_op jit(solution)/shard_map/ppermute | solution.py:47
  5.3 34.4 %collective-permute-start = (f32[19,1,8,128]{3,2,1,0:T(8,128)S(1)}, f32[19,1,8,128]{3,2,1,0:T(8,128)S(1)}, u32[]{:S(2)}, u32[]{:S(2)}) collective-permute-start(f32[19,1,8,128]{3,2,1,0:T(8,128)S(1)} %get-tuple-element.106), channel_id=1, source_target_pairs={{16,0},{32,16},{48,32},{64,48},{80,64},{96,80},{112,96},{128,112},... | collective-permute-start | bytes 233480 | tf_op jit(solution)/shard_map/ppermute | solution.py:49
  11.4 8.5 %collective-permute-start.6 = (f32[4,8,128]{2,1,0:T(8,128)S(1)}, f32[4,8,128]{2,1,0:T(8,128)S(1)}, u32[]{:S(2)}, u32[]{:S(2)}) collective-permute-start(f32[4,8,128]{2,1,0:T(8,128)S(1)} %get-tuple-element.124), channel_id=1, source_target_pairs={{0,16},{16,32},{32,48},{48,64},{64,80},{80,96},{96,112},{112,128},... | collective-permute-start | bytes 49160 | tf_op jit(solution)/shard_map/ppermute | solution.py:47
  12.7 7.5 %collective-permute-start.7 = (f32[4,8,128]{2,1,0:T(8,128)S(1)}, f32[4,8,128]{2,1,0:T(8,128)S(1)}, u32[]{:S(2)}, u32[]{:S(2)}) collective-permute-start(f32[4,8,128]{2,1,0:T(8,128)S(1)} %get-tuple-element.123), channel_id=1, source_target_pairs={{16,0},{32,16},{48,32},{64,48},{80,64},{96,80},{112,96},{128,112},... | collective-permute-start | bytes 49160 | tf_op jit(solution)/shard_map/ppermute | solution.py:49
  19.9 19.5 %copy-start.10 = (f32[19,8,8,128]{3,2,1,0:T(8,128)}, f32[19,8,8,128]{3,2,1,0:T(8,128)S(1)}, u32[]{:S(2)}) copy-start(f32[19,8,8,128]{3,2,1,0:T(8,128)S(1)} %get-tuple-element.128) | copy-start | bytes 1867780
  19.9 19.5 %copy-start.15 = (f32[19,8,8,128]{3,2,1,0:T(8,128)}, f32[19,8,8,128]{3,2,1,0:T(8,128)S(1)}, u32[]{:S(2)}) copy-start(f32[19,8,8,128]{3,2,1,0:T(8,128)S(1)} %get-tuple-element.127) | copy-start | bytes 1867780
  20.2 4.6 %collective-permute-start.8 = (f32[16,4,128]{2,1,0:T(4,128)S(1)}, f32[16,4,128]{2,1,0:T(4,128)S(1)}, u32[]{:S(2)}, u32[]{:S(2)}) collective-permute-start(f32[16,4,128]{2,1,0:T(4,128)S(1)} %get-tuple-element.116), channel_id=1, source_target_pairs={{0,4},{4,8},{8,12},{1,5},{5,9},{9,13},{2,6},{6,10},{10,14},{3,7},{... | collective-permute-start | bytes 98312 | tf_op jit(solution)/shard_map/ppermute | solution.py:47
  23.4 4.7 %collective-permute-start.9 = (f32[16,4,128]{2,1,0:T(4,128)S(1)}, f32[16,4,128]{2,1,0:T(4,128)S(1)}, u32[]{:S(2)}, u32[]{:S(2)}) collective-permute-start(f32[16,4,128]{2,1,0:T(4,128)S(1)} %get-tuple-element.117), channel_id=1, source_target_pairs={{4,0},{8,4},{12,8},{5,1},{9,5},{13,9},{6,2},{10,6},{14,10},{7,3},{... | collective-permute-start | bytes 98312 | tf_op jit(solution)/shard_map/ppermute | solution.py:49
  28.2 6.5 %collective-permute-start.10 = (f32[16,16,4]{2,1,0:T(8,128)S(1)}, f32[16,16,4]{2,1,0:T(8,128)S(1)}, u32[]{:S(2)}, u32[]{:S(2)}) collective-permute-start(f32[16,16,4]{2,1,0:T(8,128)S(1)} %get-tuple-element.111), channel_id=1, source_target_pairs={{0,1},{1,2},{2,3},{4,5},{5,6},{6,7},{8,9},{9,10},{10,11},{12,13},{... | collective-permute-start | bytes 12296 | tf_op jit(solution)/shard_map/ppermute | solution.py:47
  32.7 6.3 %collective-permute-start.11 = (f32[16,16,4]{2,1,0:T(8,128)S(1)}, f32[16,16,4]{2,1,0:T(8,128)S(1)}, u32[]{:S(2)}, u32[]{:S(2)}) collective-permute-start(f32[16,16,4]{2,1,0:T(8,128)S(1)} %get-tuple-element.112), channel_id=1, source_target_pairs={{1,0},{2,1},{3,2},{5,4},{6,5},{7,6},{9,8},{10,9},{11,10},{13,12},{... | collective-permute-start | bytes 12296 | tf_op jit(solution)/shard_map/ppermute | solution.py:49
  39.8 3.6 %collective-permute-start.2 = (f32[19,10,1,128]{3,2,1,0:T(1,128)S(1)}, f32[19,10,1,128]{3,2,1,0:T(1,128)S(1)}, u32[]{:S(2)}, u32[]{:S(2)}) collective-permute-start(f32[19,10,1,128]{3,2,1,0:T(1,128)S(1)} %get-tuple-element.62), channel_id=1, source_target_pairs={{4,0},{8,4},{12,8},{0,12},{5,1},{9,5},{13,9},{1,13},{6,2},{10,6},{... | collective-permute-start | bytes 291848 | tf_op jit(solution)/shard_map/ppermute | solution.py:49
  40.8 4.7 %collective-permute-start.3 = (f32[19,10,1,128]{3,2,1,0:T(1,128)S(1)}, f32[19,10,1,128]{3,2,1,0:T(1,128)S(1)}, u32[]{:S(2)}, u32[]{:S(2)}) collective-permute-start(f32[19,10,1,128]{3,2,1,0:T(1,128)S(1)} %get-tuple-element.61), channel_id=1, source_target_pairs={{0,4},{4,8},{8,12},{12,0},{1,5},{5,9},{9,13},{13,1},{2,6},{6,10},{... | collective-permute-start | bytes 291848 | tf_op jit(solution)/shard_map/ppermute | solution.py:47
  49.5 4.2 %collective-permute-start.4 = (f32[19,10,10,1]{0,3,2,1:T(1,128)S(1)}, f32[19,10,10,1]{0,3,2,1:T(1,128)S(1)}, u32[]{:S(2)}, u32[]{:S(2)}) collective-permute-start(f32[19,10,10,1]{0,3,2,1:T(1,128)S(1)} %copy.85), channel_id=1, source_target_pairs={{1,0},{2,1},{3,2},{0,3},{5,4},{6,5},{7,6},{4,7},{9,8},{10,9},{11,1... | collective-permute-start | bytes 22808 | tf_op jit(solution)/shard_map/ppermute | solution.py:49
  50.4 4.9 %collective-permute-start.5 = (f32[19,10,10,1]{0,3,2,1:T(1,128)S(1)}, f32[19,10,10,1]{0,3,2,1:T(1,128)S(1)}, u32[]{:S(2)}, u32[]{:S(2)}) collective-permute-start(f32[19,10,10,1]{0,3,2,1:T(1,128)S(1)} %copy.87), channel_id=1, source_target_pairs={{0,1},{1,2},{2,3},{3,0},{4,5},{5,6},{6,7},{7,4},{8,9},{9,10},{10,1... | collective-permute-start | bytes 22808 | tf_op jit(solution)/shard_map/ppermute | solution.py:47
  70.1 10.7 %collective-permute-start.12 = (f32[19,1,8,128]{3,2,1,0:T(8,128)S(1)}, f32[19,1,8,128]{3,2,1,0:T(8,128)S(1)}, u32[]{:S(2)}, u32[]{:S(2)}) collective-permute-start(f32[19,1,8,128]{3,2,1,0:T(8,128)S(1)} %get-tuple-element.85), channel_id=1, source_target_pairs={{0,16},{16,32},{32,48},{48,64},{64,80},{80,96},{96,112},{112,128},... | collective-permute-start | bytes 233480 | tf_op jit(solution)/shard_map/ppermute | solution.py:47
  74.9 7.1 %collective-permute-start.13 = (f32[19,1,8,128]{3,2,1,0:T(8,128)S(1)}, f32[19,1,8,128]{3,2,1,0:T(8,128)S(1)}, u32[]{:S(2)}, u32[]{:S(2)}) collective-permute-start(f32[19,1,8,128]{3,2,1,0:T(8,128)S(1)} %get-tuple-element.86), channel_id=1, source_target_pairs={{16,0},{32,16},{48,32},{64,48},{80,64},{96,80},{112,96},{128,112},... | collective-permute-start | bytes 233480 | tf_op jit(solution)/shard_map/ppermute | solution.py:49
  82.1 5.2 %collective-permute-start.14 = (f32[19,10,1,128]{3,2,1,0:T(1,128)S(1)}, f32[19,10,1,128]{3,2,1,0:T(1,128)S(1)}, u32[]{:S(2)}, u32[]{:S(2)}) collective-permute-start(f32[19,10,1,128]{3,2,1,0:T(1,128)S(1)} %get-tuple-element.59), channel_id=1, source_target_pairs={{0,4},{4,8},{8,12},{12,0},{1,5},{5,9},{9,13},{13,1},{2,6},{6,10},{... | collective-permute-start | bytes 291848 | tf_op jit(solution)/shard_map/ppermute | solution.py:47
  82.1 5.2 %collective-permute-start.15 = (f32[19,10,1,128]{3,2,1,0:T(1,128)S(1)}, f32[19,10,1,128]{3,2,1,0:T(1,128)S(1)}, u32[]{:S(2)}, u32[]{:S(2)}) collective-permute-start(f32[19,10,1,128]{3,2,1,0:T(1,128)S(1)} %get-tuple-element.60), channel_id=1, source_target_pairs={{4,0},{8,4},{12,8},{0,12},{5,1},{9,5},{13,9},{1,13},{6,2},{10,6},{... | collective-permute-start | bytes 291848 | tf_op jit(solution)/shard_map/ppermute | solution.py:49
  93.3 3.3 %collective-permute-start.16 = (f32[19,10,10,1]{0,3,2,1:T(1,128)}, f32[19,10,10,1]{0,3,2,1:T(1,128)}, u32[]{:S(2)}, u32[]{:S(2)}) collective-permute-start(f32[19,10,10,1]{0,3,2,1:T(1,128)} %copy.89), channel_id=1, source_target_pairs={{0,1},{1,2},{2,3},{3,0},{4,5},{5,6},{6,7},{7,4},{8,9},{9,10},{10,1... | collective-permute-start | bytes 22808 | tf_op jit(solution)/shard_map/ppermute | solution.py:47
  95.2 3.9 %collective-permute-start.17 = (f32[19,10,10,1]{0,3,2,1:T(1,128)}, f32[19,10,10,1]{0,3,2,1:T(1,128)}, u32[]{:S(2)}, u32[]{:S(2)}) collective-permute-start(f32[19,10,10,1]{0,3,2,1:T(1,128)} %copy.91), channel_id=1, source_target_pairs={{1,0},{2,1},{3,2},{0,3},{5,4},{6,5},{7,6},{4,7},{9,8},{10,9},{11,1... | collective-permute-start | bytes 22808 | tf_op jit(solution)/shard_map/ppermute | solution.py:49
  107.0 7.1 %collective-permute-start.18 = (f32[19,1,8,128]{3,2,1,0:T(8,128)S(1)}, f32[19,1,8,128]{3,2,1,0:T(8,128)S(1)}, u32[]{:S(2)}, u32[]{:S(2)}) collective-permute-start(f32[19,1,8,128]{3,2,1,0:T(8,128)S(1)} %get-tuple-element.66), channel_id=1, source_target_pairs={{16,0},{32,16},{48,32},{64,48},{80,64},{96,80},{112,96},{128,112},... | collective-permute-start | bytes 233480 | tf_op jit(solution)/shard_map/ppermute | solution.py:49
  112.7 6.9 %collective-permute-start.19 = (f32[19,1,8,128]{3,2,1,0:T(8,128)S(1)}, f32[19,1,8,128]{3,2,1,0:T(8,128)S(1)}, u32[]{:S(2)}, u32[]{:S(2)}) collective-permute-start(f32[19,1,8,128]{3,2,1,0:T(8,128)S(1)} %get-tuple-element.65), channel_id=1, source_target_pairs={{0,16},{16,32},{32,48},{48,64},{64,80},{80,96},{96,112},{112,128},... | collective-permute-start | bytes 233480 | tf_op jit(solution)/shard_map/ppermute | solution.py:47
  119.7 4.4 %collective-permute-start.20 = (f32[19,10,1,128]{3,2,1,0:T(1,128)S(1)}, f32[19,10,1,128]{3,2,1,0:T(1,128)S(1)}, u32[]{:S(2)}, u32[]{:S(2)}) collective-permute-start(f32[19,10,1,128]{3,2,1,0:T(1,128)S(1)} %get-tuple-element.58), channel_id=1, source_target_pairs={{4,0},{8,4},{12,8},{0,12},{5,1},{9,5},{13,9},{1,13},{6,2},{10,6},{... | collective-permute-start | bytes 291848 | tf_op jit(solution)/shard_map/ppermute | solution.py:49
  122.4 4.7 %collective-permute-start.21 = (f32[19,10,1,128]{3,2,1,0:T(1,128)S(1)}, f32[19,10,1,128]{3,2,1,0:T(1,128)S(1)}, u32[]{:S(2)}, u32[]{:S(2)}) collective-permute-start(f32[19,10,1,128]{3,2,1,0:T(1,128)S(1)} %get-tuple-element.57), channel_id=1, source_target_pairs={{0,4},{4,8},{8,12},{12,0},{1,5},{5,9},{9,13},{13,1},{2,6},{6,10},{... | collective-permute-start | bytes 291848 | tf_op jit(solution)/shard_map/ppermute | solution.py:47
  131.3 5.1 %collective-permute-start.22 = (f32[19,10,10,1]{0,3,2,1:T(1,128)S(1)}, f32[19,10,10,1]{0,3,2,1:T(1,128)S(1)}, u32[]{:S(2)}, u32[]{:S(2)}) collective-permute-start(f32[19,10,10,1]{0,3,2,1:T(1,128)S(1)} %copy.93), channel_id=1, source_target_pairs={{1,0},{2,1},{3,2},{0,3},{5,4},{6,5},{7,6},{4,7},{9,8},{10,9},{11,1... | collective-permute-start | bytes 22808 | tf_op jit(solution)/shard_map/ppermute | solution.py:49
  134.7 3.2 %collective-permute-start.23 = (f32[19,10,10,1]{0,3,2,1:T(1,128)S(1)}, f32[19,10,10,1]{0,3,2,1:T(1,128)S(1)}, u32[]{:S(2)}, u32[]{:S(2)}) collective-permute-start(f32[19,10,10,1]{0,3,2,1:T(1,128)S(1)} %copy.95), channel_id=1, source_target_pairs={{0,1},{1,2},{2,3},{3,0},{4,5},{5,6},{6,7},{7,4},{8,9},{9,10},{10,1... | collective-permute-start | bytes 22808 | tf_op jit(solution)/shard_map/ppermute | solution.py:47
  153.3 2.6 collective-permute-start.24
  154.6 6.0 %collective-permute-start.25 = (f32[4,8,128]{2,1,0:T(8,128)S(1)}, f32[4,8,128]{2,1,0:T(8,128)S(1)}, u32[]{:S(2)}, u32[]{:S(2)}) collective-permute-start(f32[4,8,128]{2,1,0:T(8,128)S(1)} %get-tuple-element.120), channel_id=1, source_target_pairs={{16,0},{32,16},{48,32},{64,48},{80,64},{96,80},{112,96},{128,112},... | collective-permute-start | bytes 49160 | tf_op jit(solution)/shard_map/ppermute | solution.py:49
  160.6 2.6 collective-permute-start.26
  161.9 4.7 %collective-permute-start.27 = (f32[16,4,128]{2,1,0:T(4,128)S(1)}, f32[16,4,128]{2,1,0:T(4,128)S(1)}, u32[]{:S(2)}, u32[]{:S(2)}) collective-permute-start(f32[16,4,128]{2,1,0:T(4,128)S(1)} %get-tuple-element.115), channel_id=1, source_target_pairs={{4,0},{8,4},{12,8},{5,1},{9,5},{13,9},{6,2},{10,6},{14,10},{7,3},{... | collective-permute-start | bytes 98312 | tf_op jit(solution)/shard_map/ppermute | solution.py:49
  166.7 6.8 %collective-permute-start.28 = (f32[16,16,4]{2,1,0:T(8,128)S(1)}, f32[16,16,4]{2,1,0:T(8,128)S(1)}, u32[]{:S(2)}, u32[]{:S(2)}) collective-permute-start(f32[16,16,4]{2,1,0:T(8,128)S(1)} %get-tuple-element.107), channel_id=1, source_target_pairs={{0,1},{1,2},{2,3},{4,5},{5,6},{6,7},{8,9},{9,10},{10,11},{12,13},{... | collective-permute-start | bytes 12296 | tf_op jit(solution)/shard_map/ppermute | solution.py:47
  171.6 6.3 %collective-permute-start.29 = (f32[16,16,4]{2,1,0:T(8,128)S(1)}, f32[16,16,4]{2,1,0:T(8,128)S(1)}, u32[]{:S(2)}, u32[]{:S(2)}) collective-permute-start(f32[16,16,4]{2,1,0:T(8,128)S(1)} %get-tuple-element.108), channel_id=1, source_target_pairs={{1,0},{2,1},{3,2},{5,4},{6,5},{7,6},{9,8},{10,9},{11,10},{13,12},{... | collective-permute-start | bytes 12296 | tf_op jit(solution)/shard_map/ppermute | solution.py:49
  (44 other events, 126.5 us)
where the time goes:
time: 268 us; the launch traced here: 266 us
  blocking collectives  85 us (32%)
  starting transfers between devices  62.2 us (23%)
  local copies, waits for them, and re-layouts  41.5 us (15%)
  other arithmetic  37.6 us (14%)
  waiting for transfers between devices  36 us (13%)
  between operations  4.25 us (2%)
    psum x1, blocking collectives, body(): squares = lax.psum(jnp.sum(raw_grad * raw_grad), ('gx', 'gy', 'gz'))  85 us
    ppermute x15, starting transfers between devices, with_halo(): lax.ppermute(head, axis, [((i + 1) % count, i) for i in range(ends)])  34.1 us
    ppermute x15, starting transfers between devices, with_halo(): lax.ppermute(tail, axis, [(i, (i + 1) % count) for i in range(ends)])  28.1 us
    ppermute x15, waiting for transfers between devices, with_halo(): lax.ppermute(head, axis, [((i + 1) % count, i) for i in range(ends)])  23.3 us
    unnamed x68, other arithmetic  22.9 us
    ppermute x15, waiting for transfers between devices, with_halo(): lax.ppermute(tail, axis, [(i, (i + 1) % count) for i in range(ends)])  12.7 us
    slice x14, local copies, waits for them, and re-layouts, with_halo(): lax.slice_in_dim(cells, cells.shape[dim] - width, cells.shape[dim], axis=...  9.1 us
    unnamed x170, local copies, waits for them, and re-layouts  9.06 us
  transfers between devices with their start and end apart: 30, of which 16 were waited for; matrix products, arithmetic and copies ran while one was open for 9% of the time, Pallas kernels for 0%

commit v1 on v0

v1 whole, which is shorter than its diff:
```python
import functools

import jax
import jax.numpy as jnp
import numpy as np
from jax import lax
from jax.experimental import pallas as pl
from jax.experimental.pallas import tpu as pltpu
from jax.sharding import PartitionSpec as P

MESH = pl.DeviceIdType.MESH
F32 = jnp.float32
BF16 = jnp.bfloat16

velocities = [
    (0, 0, 0),
    (1, 0, 0),
    (-1, 0, 0),
    (0, 1, 0),
    (0, -1, 0),
    (0, 0, 1),
    (0, 0, -1),
    (1, 1, 0),
    (-1, -1, 0),
    (1, -1, 0),
    (-1, 1, 0),
    (1, 0, 1),
    (-1, 0, -1),
    (1, 0, -1),
    (-1, 0, 1),
    (0, 1, 1),
    (0, -1, -1),
    (0, 1, -1),
    (0, -1, 1),
]
opposite = [0, 2, 1, 4, 3, 6, 5, 8, 7, 10, 9, 12, 11, 14, 13, 16, 15, 18, 17]
pair_weights = [1.0 / 18.0] * 3 + [1.0 / 36.0] * 6
relax_rate = 1.6
inlet_speed = 0.05
norm_eps = 1e-06
FAR = 4096.0

crossing = {
    (0, 1): [1, 7, 9, 11, 13],
    (0, -1): [2, 8, 10, 12, 14],
    (1, 1): [3, 7, 10, 15, 17],
    (1, -1): [4, 8, 9, 16, 18],
    (2, 1): [5, 11, 14, 15, 18],
    (2, -1): [6, 12, 13, 16, 17],
}
side = {1: 0, -1: 1}
kind = {0: 0, 1: 1, -1: 2}

regions = {(0, 0): (0, 64)}
for order, where_ in enumerate([(-1, 0), (1, 0), (0, -1), (0, 1), (-1, -1), (-1, 1), (1, -1), (1, 1)]):
    regions[where_] = (64 + 40 * order, 40)

flows = [
    (a, b, c) for a in (1, -1, 0) for b in (1, -1, 0) for c in (1, -1, 0) if a or b or c
]
flow_index = {flow: number for number, flow in enumerate(flows)}


def lane_table():
    table = np.zeros((8, 384), np.float32)
    for (a, b), (start, rows) in regions.items():
        for r in range(rows):
            tile, sub = divmod(r, 8)
            if (a, b) == (0, 0):
                x, y = tile, sub
            elif b == 0:
                x, y = (tile - 5 if a < 0 else tile + 8), sub
            else:
                y = tile - 5 if b < 0 else tile + 8
                x = sub + 8 * a
            table[0, start + r] = x
            table[1, start + r] = y
    lanes = np.arange(384)
    table[2] = np.where(lanes < 128, lanes, np.where(lanes < 256, lanes - 129, lanes - 255))
    block = np.arange(256) // 16
    table[3, :256] = np.where(block < 10, block - 1, 3 * FAR)
    table[4, :256] = np.arange(256) % 16
    table[5, :128] = np.where(np.arange(128) < 24, np.arange(128) - 8, 3 * FAR)
    return table


def split(value):
    high = value.astype(BF16)
    return high, (value - high.astype(F32)).astype(BF16)


def left_dot(matrix, value):
    high, low = split(value)
    return jnp.dot(matrix, high, preferred_element_type=F32) + jnp.dot(
        matrix, low, preferred_element_type=F32
    )


def right_dot(value, matrix):
    high, low = split(value)
    return jnp.dot(high, matrix, preferred_element_type=F32) + jnp.dot(
        low, matrix, preferred_element_type=F32
    )


def right_dot_t(value, matrix):
    high, low = split(value)
    dims = (((1,), (1,)), ((), ()))
    return lax.dot_general(high, matrix, dims, preferred_element_type=F32) + lax.dot_general(
        low, matrix, dims, preferred_element_type=F32
    )


def triangle(n):
    return 0.5 * n * (n + 1.0)


def weight_total(position, count):
    position = jnp.where(position < 0, position + count, position)
    position = jnp.where(position > count - 1, position - count, position)
    return (
        25.0
        - triangle(jnp.maximum(0.0, 4.0 - position))
        - triangle(jnp.maximum(0.0, position - (count - 5.0)))
    )


def cut(value, last, low, high):
    return (
        value
        - jnp.where(value < 0, FAR, 0.0) * low
        + jnp.where(value > last, FAR, 0.0) * high
    )


def hat(difference):
    return jnp.maximum(0.0, 5.0 - jnp.abs(difference))


def add_all(terms):
    terms = list(terms)
    while len(terms) > 1:
        terms = [
            terms[n] + terms[n + 1] if n + 1 < len(terms) else terms[n]
            for n in range(0, len(terms), 2)
        ]
    return terms[0]


def project(c, vector):
    total = None
    for component, value in zip(c, vector):
        if component == 1:
            total = value if total is None else total + value
        elif component == -1:
            total = -value if total is None else total - value
    return total


def momentum(t):
    return (
        add_all([t[0], t[3] + t[4], t[5] + t[6]]),
        add_all([t[1], t[3] - t[4], t[7] + t[8]]),
        add_all([t[2], t[5] - t[6], t[7] - t[8]]),
    )


def cell_kinds(flags):
    omega = jnp.where(flags == 3, 1.0, relax_rate)
    solid = flags == 1
    inlet = flags == 2
    blocked = jnp.logical_or(solid, inlet)
    keep = 1.0 - omega
    even = jnp.where(solid, 1.0, jnp.where(inlet, 0.0, keep))
    odd = jnp.where(solid, -1.0, jnp.where(inlet, 0.0, keep))
    fluid_omega = jnp.where(blocked, 0.0, omega)
    return omega, keep, solid, inlet, blocked, even, odd, fluid_omega


def first_collision(f, flags):
    omega, keep, solid, inlet, blocked, even, odd, fluid_omega = cell_kinds(flags)
    rate = jnp.where(inlet, 1.0, fluid_omega)
    s = [f[2 * p + 1] + f[2 * p + 2] for p in range(9)]
    t = [f[2 * p + 1] - f[2 * p + 2] for p in range(9)]
    rho = jnp.where(inlet, 1.0, add_all([f[0]] + s))
    mx, my, mz = momentum(t)
    mx = jnp.where(inlet, inlet_speed, mx)
    my = jnp.where(inlet, 0.0, my)
    mz = jnp.where(inlet, 0.0, mz)
    inverse = 1.0 / rho
    base = rho - 1.5 * (mx * mx + my * my + mz * mz) * inverse
    bend = 4.5 * inverse
    half_even, half_odd = 0.5 * even, 0.5 * odd
    base_a, base_b = rate * pair_weights[0], rate * pair_weights[3]
    first = [even * f[0] + rate * (1.0 / 3.0) * base]
    slope = []
    for p in range(9):
        along = project(velocities[2 * p + 1], (mx, my, mz))
        weight = base_a if p < 3 else base_b
        symmetric = half_even * s[p] + weight * (base + bend * (along * along))
        skew = half_odd * t[p] + (3.0 * weight) * along
        first += [symmetric + skew, symmetric - skew]
        slope.append(jnp.where(blocked, 0.0, -2.0 * skew))
    return first, slope


def adjoint_collision(f, a, kappa, flags):
    omega, keep, solid, inlet, blocked, even, odd, fluid_omega = cell_kinds(flags)
    pass_back = 1.0 - 2.0 * kappa
    s = [f[2 * p + 1] + f[2 * p + 2] for p in range(9)]
    t = [f[2 * p + 1] - f[2 * p + 2] for p in range(9)]
    rho = add_all([f[0]] + s)
    mx, my, mz = momentum(t)
    inverse = 1.0 / rho
    ux, uy, uz = mx * inverse, my * inverse, mz * inverse
    even_a = [a[2 * p + 1] + a[2 * p + 2] for p in range(9)]
    odd_a = [a[2 * p + 1] - a[2 * p + 2] for p in range(9)]
    ws = [pair_weights[p] * even_a[p] for p in range(9)]
    wt = [pair_weights[p] * odd_a[p] for p in range(9)]
    b0 = add_all([(1.0 / 3.0) * a[0]] + ws)
    b1x, b1y, b1z = momentum(wt)
    bxx = add_all([ws[0], ws[3] + ws[4], ws[5] + ws[6]])
    byy = add_all([ws[1], ws[3] + ws[4], ws[7] + ws[8]])
    bzz = add_all([ws[2], ws[5] + ws[6], ws[7] + ws[8]])
    bxy, bxz, byz = ws[3] - ws[4], ws[5] - ws[6], ws[7] - ws[8]
    vx = bxx * ux + bxy * uy + bxz * uz
    vy = bxy * ux + byy * uy + byz * uz
    vz = bxz * ux + byz * uy + bzz * uz
    moved = 3.0 * (mx * b1x + my * b1y + mz * b1z)
    kept = add_all([odd_a[p] * t[p] for p in range(9)])
    slope = jnp.where(blocked, 0.0, -(keep * kept + 2.0 * omega * moved))
    usq = ux * ux + uy * uy + uz * uz
    to_rho = fluid_omega * (b0 * (1.0 + 1.5 * usq) - 4.5 * (ux * vx + uy * vy + uz * vz))
    back = 3.0 * pass_back
    gx = fluid_omega * (back * b1x + 9.0 * vx - 3.0 * ux * b0)
    gy = fluid_omega * (back * b1y + 9.0 * vy - 3.0 * uy * b0)
    gz = fluid_omega * (back * b1z + 9.0 * vz - 3.0 * uz * b0)
    half_even = 0.5 * even
    half_odd = 0.5 * jnp.where(blocked, odd, odd * pass_back)
    result = [even * a[0] + to_rho]
    for p in range(9):
        along = project(velocities[2 * p + 1], (gx, gy, gz))
        symmetric = half_even * even_a[p] + to_rho
        skew = half_odd * odd_a[p] + along
        result += [symmetric + skew, symmetric - skew]
    return result, slope


def aligned(index):
    return pl.multiple_of(index * 8, 8)


def kernel(
    sizes,
    pop_in,
    design_in,
    flags_in,
    seed_in,
    table_in,
    out_ref,
    rms_ref,
    pops,
    flags_v,
    table,
    first_v,
    slope_v,
    seed_v,
    field,
    x_send,
    x_recv,
    y_field,
    y_send,
    y_rows,
    xy_send,
    z_send,
    z_recv,
    z_pack,
    kappa_v,
    grad_v,
    spread,
    spread_recv,
    q_out,
    q_recv,
    ring_a,
    ring_b,
    big_l,
    big_l_wide,
    big_lt,
    rep_l,
    rep_l_wide,
    rep_lt,
    cross_x,
    cross_z,
    block_mask,
    row_scale,
    local_sem,
    send_sem,
    recv_sem,
):
    nx, ny, nz = sizes
    gx, gy, gz = lax.axis_index("gx"), lax.axis_index("gy"), lax.axis_index("gz")

    def device(move):
        return (
            lax.rem(gx + move[0] % nx, nx),
            lax.rem(gy + move[1] % ny, ny),
            lax.rem(gz + move[2] % nz, nz),
        )

    slab_moves = [(0, b, c) for b in range(ny) for c in range(nz) if b or c]
    slab_moves.sort(key=lambda m: -(min(m[1], ny - m[1]) + min(m[2], nz - m[2])))
    line_moves = [(a, 0, 2 * (a % 2)) for a in range(1, nx)]
    line_moves.sort(key=lambda m: -(min(m[0], nx - m[0]) + 2 * (m[0] % 2)))

    def key(move):
        return (move[0] % nx, move[1] % ny, move[2] % nz)

    partners = []
    for move in line_moves + flows + slab_moves:
        if key(move) not in partners:
            partners.append(key(move))
    barrier = pltpu.get_barrier_semaphore()
    for move in partners:
        pl.semaphore_signal(barrier, inc=1, device_id=device(move), device_id_type=MESH)

    loads = [
        pltpu.make_async_copy(table_in, table, local_sem.at[0]),
        pltpu.make_async_copy(pop_in, pops, local_sem.at[1]),
        pltpu.make_async_copy(flags_in, flags_v, local_sem.at[2]),
        pltpu.make_async_copy(seed_in, seed_v.at[:, pl.ds(8, 64), :], local_sem.at[3]),
        pltpu.make_async_copy(design_in, field.at[pl.ds(0, 64)], local_sem.at[4]),
    ]
    for load in loads:
        load.start()
    for load in loads:
        load.wait()

    lane = lax.broadcasted_iota(jnp.int32, (8, 128), 1)
    row = lax.broadcasted_iota(jnp.int32, (8, 128), 0)

    def own(k, j, rows):
        if k == 0:
            return first_v[j, rows, :]
        if k == 1:
            return slope_v[(j - 1) // 2, rows, :]
        return seed_v[opposite[j], rows, :]

    def start_step(x, carry):
        rows = pl.ds(aligned(x), 8)
        inner = pl.ds(aligned(x + 1), 8)
        first, slope = first_collision([pops[i, rows, :] for i in range(19)], flags_v[rows, :])
        for i in range(19):
            first_v[i, inner, :] = first[i]
        for p in range(9):
            slope_v[p, inner, :] = slope[p]
        packs = list(carry[:2])
        for n, sign in enumerate((1, -1)):
            edge = 127 if sign == 1 else 0
            for k in range(3):
                for s, j in enumerate(crossing[2, sign]):
                    tile = (
                        first[j]
                        if k == 0
                        else slope[(j - 1) // 2]
                        if k == 1
                        else seed_v[opposite[j], inner, :]
                    )
                    place = k * 40 + s * 8 + x
                    moved = pltpu.roll(tile, jnp.bitwise_and(place + 128 - edge, 127), 1)
                    packs[n] = jnp.where(lane == place, moved, packs[n])
        tile = field[rows, :]
        quad = carry[2]
        here = lax.shift_right_logical(lane, 4) == x
        part = jnp.bitwise_and(lane, 15)
        high = pltpu.roll(tile, jnp.bitwise_and(16 * x + 5, 127), 1)
        low = pltpu.roll(tile, jnp.bitwise_and(16 * x + 8, 127), 1)
        quad = jnp.where(jnp.logical_and(here, part < 5), high, quad)
        quad = jnp.where(
            jnp.logical_and(here, jnp.logical_and(part >= 8, part < 13)), low, quad
        )
        return packs[0], packs[1], quad

    blank = jnp.zeros((8, 128), F32)
    pack_up, pack_down, quad = lax.fori_loop(0, 8, start_step, (blank, blank, blank))
    z_send[0, 0] = quad
    z_send[1, 0] = quad
    z_send[0, 1] = pack_up
    z_send[1, 1] = pack_down
    for sign in (1, -1):
        n = side[sign]
        edge = 7 if sign == 1 else 0
        for k in range(3):
            for s, j in enumerate(crossing[0, sign]):
                x_send[n, 5 * k + s] = own(k, j, pl.ds(8 * (edge + 1), 8))
            for s, j in enumerate(crossing[1, sign]):
                y_send[n, 5 * k + s] = own(k, j, pl.ds(8 + edge, 8, stride=8))
        for r in range(5):
            y_field[n, pl.ds(8 * r, 8), :] = field[
                pl.ds(3 + r if sign == 1 else r, 8, stride=8), :
            ]
    diagonals = [(a, b) for a in (1, -1) for b in (1, -1)]
    for n, (a, b) in enumerate(diagonals):
        j = velocities.index((a, b, 0))
        xy_send[n] = y_field[side[b]]
        for k in range(3):
            at = (8 if a == 1 else 1) * 8 + (7 if b == 1 else 0)
            xy_send[n, pl.ds(k if a == 1 else 5 + k, 1), :] = own(k, j, pl.ds(at, 1))

    def one_if(condition):
        return jnp.where(condition, 1.0, 0.0).astype(F32)

    x_low, x_high = one_if(gx == 0), one_if(gx == nx - 1)
    y_low, y_high = one_if(gy == 0), one_if(gy == ny - 1)
    z_low, z_high = one_if(gz == 0), one_if(gz == nz - 1)
    lanes_x = cut(table[0:1, :], 7.0, x_low, x_high)
    lanes_y = cut(table[1:2, :], 7.0, y_low, y_high)
    lanes_z = cut(table[2:3, :], 127.0, z_low, z_high)
    blocks_x = cut(table[3:4, 0:256], 7.0, x_low, x_high)
    blocks_part = table[4:5, 0:256]
    stack_y = cut(table[5:6, 0:128], 7.0, y_low, y_high)
    lane_scale = 1.0 / weight_total(
        table[2:3, :] + (gz * 128).astype(F32), 128.0 * nz
    )

    def build_rows(t, carry):
        rows = pl.ds(pl.multiple_of(t * 16, 16), 16)
        index = lax.broadcasted_iota(jnp.int32, (16, 128), 0) + t * 16
        tile = lax.shift_right_logical(index, 3)
        late = jnp.where(tile >= 20, 2, jnp.where(tile >= 10, 1, 0))
        plane = tile - 10 * late
        x = (plane - 1).astype(F32)
        y = (jnp.bitwise_and(index, 7) - jnp.where(late == 1, 1, jnp.where(late == 2, -1, 0))).astype(F32)
        row_scale[rows, :] = 1.0 / (
            weight_total(x + (gx * 8).astype(F32), 8.0 * nx)
            * weight_total(y + (gy * 8).astype(F32), 8.0 * ny)
        )
        cut_x = cut(x, 7.0, x_low, x_high)
        cut_y = cut(y, 7.0, y_low, y_high)
        wide_x = jnp.concatenate([cut_x] * 3, axis=1)
        wide_y = jnp.concatenate([cut_y] * 3, axis=1)
        weights = hat(wide_x - lanes_x) * hat(wide_y - lanes_y)
        big_l_wide[rows, :] = weights
        big_l[rows, :] = weights.astype(BF16)
        repeated = hat(cut_y - stack_y)
        rep_l_wide[rows, :] = repeated
        rep_l[rows, :] = repeated.astype(BF16)
        block = lax.shift_right_logical(lax.broadcasted_iota(jnp.int32, (16, 256), 1), 4)
        block_mask[rows, :] = jnp.where(
            block == jnp.concatenate([plane] * 2, axis=1), 1.0, 0.0
        )
        return carry

    lax.fori_loop(0, 16, build_rows, 0)
    big_lt[...] = big_l_wide[...].T.astype(BF16)
    rep_lt[...] = rep_l_wide[...].T[0:32, :].astype(BF16)

    def build_cross(t, carry):
        rows = pl.ds(pl.multiple_of(t * 16, 16), 16)
        x = cut((t - 8).astype(F32), 7.0, x_low, x_high)
        same = lax.broadcasted_iota(jnp.int32, (16, 256), 0).astype(F32) == blocks_part
        cross_x[rows, :] = jnp.where(same, hat(x - blocks_x), 0.0).astype(BF16)
        return carry

    lax.fori_loop(0, 24, build_cross, 0)

    def build_z(t, carry):
        rows = pl.ds(pl.multiple_of(t * 16, 16), 16)
        index = lax.broadcasted_iota(jnp.int32, (16, 384), 0)
        inside = index + t * 16
        halo = jnp.where(
            index < 5,
            index - 5,
            jnp.where(jnp.logical_and(index >= 8, index < 13), index + 120, 100000),
        )
        z = cut(jnp.where(t < 8, inside, halo).astype(F32), 127.0, z_low, z_high)
        cross_z[rows, :] = hat(z - lanes_z).astype(BF16)
        return carry

    lax.fori_loop(0, 24, build_z, 0)
    grad_v[...] = jnp.zeros_like(grad_v)

    pl.semaphore_wait(barrier, len(partners))
    count = [0]
    started = []

    def send(source, target, move):
        n = count[0]
        count[0] += 1
        copy = pltpu.make_async_remote_copy(
            src_ref=source,
            dst_ref=target,
            send_sem=send_sem.at[n],
            recv_sem=recv_sem.at[n],
            device_id=device(move),
            device_id_type=MESH,
        )
        copy.start()
        started.append(copy)
        return copy

    def region(a, b):
        start, rows = regions[a, b]
        return pl.ds(start, rows)

    field_copies, fill_copies = [], []
    for n, (a, b) in enumerate(diagonals):
        field_copies.append(send(xy_send.at[n], field.at[region(-a, -b)], (a, b, 0)))
    for a in (1, -1):
        source = pl.ds(24, 40) if a == 1 else pl.ds(0, 40)
        field_copies.append(send(field.at[source], field.at[region(-a, 0)], (a, 0, 0)))
    for flow in flows:
        if flow[2] != 0:
            n = flow_index[flow]
            if flow[0] != 0 and flow[1] != 0:
                source, target = z_send.at[side[flow[2]], 0], z_recv.at[n, 0]
            else:
                source, target = z_send.at[side[flow[2]]], z_recv.at[n]
            field_copies.append(send(source, target, flow))
    for b in (1, -1):
        field_copies.append(send(y_field.at[side[b]], field.at[region(0, -b)], (0, b, 0)))
    for a in (1, -1):
        fill_copies.append(send(x_send.at[side[a]], x_recv.at[side[a]], (a, 0, 0)))
    for b in (1, -1):
        fill_copies.append(
            send(y_send.at[side[b]], y_rows.at[side[b], :, pl.ds(8, 8), :], (0, b, 0))
        )

    for copy in field_copies:
        copy.wait_recv()
    inner_xy = left_dot(big_l[...], field[...])
    part = jnp.bitwise_and(lane, 15)
    stacked = []
    for b in (-1, 0, 1):
        tiles = []
        for a in (-1, 0, 1):
            below = z_recv[flow_index[-a, -b, 1], 0]
            above = z_recv[flow_index[-a, -b, -1], 0]
            tiles.append(jnp.where(part < 8, below, above))
        stacked.append(jnp.concatenate(tiles, axis=1))
    stacked.append(jnp.zeros((8, 384), F32))
    halo_x = right_dot(jnp.concatenate(stacked, axis=0), cross_x[...])
    halo_x = jnp.concatenate([halo_x, jnp.zeros((96, 256), F32)], axis=0)
    halo_xy = left_dot(rep_l[...], halo_x) * block_mask[...]
    summed = right_dot(jnp.concatenate([inner_xy, halo_xy], axis=1), cross_z[...])
    scale_rows = jnp.concatenate([row_scale[...]] * 3, axis=1)
    kappa_v[...] = 0.5 * (1.0 - summed * scale_rows * lane_scale)

    for copy in fill_copies:
        copy.wait_recv()
    for sign in (1, -1):
        n = side[sign]
        rows = pl.ds(0, 8) if sign == 1 else pl.ds(72, 8)
        for s, j in enumerate(crossing[0, sign]):
            first_v[j, rows, :] = x_recv[n, s]
            slope_v[(j - 1) // 2, rows, :] = x_recv[n, 5 + s]
            seed_v[opposite[j], rows, :] = x_recv[n, 10 + s]
    for a, b in diagonals:
        j = velocities.index((a, b, 0))
        s = crossing[1, b].index(j)
        start = regions[-a, -b][0]
        for k in range(3):
            y_rows[side[b], 5 * k + s, pl.ds(7 if a == 1 else 16, 1), :] = field[
                pl.ds(start + (k if a == 1 else 5 + k), 1), :
            ]
    eighth = lax.shift_right_logical(lane, 3)
    slot = eighth - jnp.where(eighth >= 10, 10, jnp.where(eighth >= 5, 5, 0))
    step = jnp.bitwise_and(lane, 7)
    for sign in (1, -1):
        base = z_recv[flow_index[0, 0, sign], 1]
        total = base
        for s, j in enumerate(crossing[2, sign]):
            a, b, _ = velocities[j]
            if a != 0:
                corner = z_recv[flow_index[a, 0, sign], 1]
                if a == 1:
                    moved = jnp.where(step == 0, pltpu.roll(corner, 121, 1), pltpu.roll(base, 1, 1))
                else:
                    moved = jnp.where(step == 7, pltpu.roll(corner, 7, 1), pltpu.roll(base, 127, 1))
            elif b != 0:
                corner = z_recv[flow_index[0, b, sign], 1]
                if b == 1:
                    moved = pltpu.roll(jnp.where(row == 7, corner, base), 1, 0)
                else:
                    moved = pltpu.roll(jnp.where(row == 0, corner, base), 7, 0)
            else:
                continue
            total = jnp.where(slot == s, moved, total)
        z_pack[side[sign]] = total

    def plane_step(x, carry):
        def stream(k, j):
            a, b, c = velocities[j]
            tile = own(k, j, pl.ds(aligned(x + 1 - a), 8))
            if b != 0:
                s = crossing[1, b].index(j)
                line = y_rows[side[b], 5 * k + s, pl.ds(8 + x - a, 1), :]
                tile = jnp.where(
                    row == (0 if b == 1 else 7), line, pltpu.roll(tile, b % 8, 0)
                )
            if c != 0:
                s = crossing[2, c].index(j)
                edge = 0 if c == 1 else 127
                place = k * 40 + s * 8 + x
                column = pltpu.roll(
                    z_pack[side[c]], jnp.bitwise_and(256 + edge - place, 127), 1
                )
                tile = jnp.where(lane == edge, column, pltpu.roll(tile, c % 128, 1))
            return tile

        def spot(j):
            a, b, c = velocities[j]
            return (
                pl.ds(aligned(kind[b] * 10 + x + 1 - a), 8),
                pl.ds(128 * kind[c], 128),
            )

        center = pl.ds(aligned(x + 1), 8)
        flags = flags_v[pl.ds(aligned(x), 8), :]
        state, slopes = [first_v[0, center, :]], [None]
        weights = [seed_v[0, center, :]] + [None] * 18
        for j in range(1, 19):
            slope = stream(1, j)
            rows, lanes = spot(j)
            change = kappa_v[rows, lanes] * slope
            before = stream(0, j)
            state.append(before + change if j % 2 == 1 else before - change)
            slopes.append(slope)
            weights[opposite[j]] = stream(2, j)
        kappa = kappa_v[center, 0:128]
        back, here = adjoint_collision(state, weights, kappa, flags)
        grad_v[center, 0:128] += here
        for j in range(1, 19):
            rows, lanes = spot(j)
            if j % 2 == 1:
                grad_v[rows, lanes] += slopes[j] * back[j]
            else:
                grad_v[rows, lanes] -= slopes[j] * back[j]
        return carry

    lax.fori_loop(0, 8, plane_step, 0)

    scaled = grad_v[...] * (scale_rows * (-0.5 * lane_scale))
    summed = right_dot_t(scaled, cross_z[...])
    spread[...] = left_dot(big_lt[...], summed[:, 0:128])
    halo_x = left_dot(rep_lt[...], summed[:, 128:384] * block_mask[...])
    halo = right_dot_t(halo_x, cross_x[...])
    for b in range(3):
        for a in range(3):
            q_out[3 * b + a] = halo[8 * b : 8 * b + 8, 128 * a : 128 * a + 128]
    spread_copies = []
    for flow in flows:
        a, b, c = flow
        if c == 0:
            spread_copies.append(
                send(spread.at[region(a, b)], spread_recv.at[region(a, b)], flow)
            )
        else:
            spread_copies.append(
                send(q_out.at[3 * (b + 1) + a + 1], q_recv.at[flow_index[flow]], flow)
            )
    for copy in spread_copies:
        copy.wait_recv()
    spread[pl.ds(24, 40), :] += spread_recv[region(-1, 0), :]
    spread[pl.ds(0, 40), :] += spread_recv[region(1, 0), :]
    for b in (1, -1):
        lines = (
            spread_recv[region(0, b), :]
            + spread_recv[region(-1, b), :]
            + spread_recv[region(1, b), :]
        )
        for r in range(5):
            at = pl.ds(r if b == 1 else 3 + r, 8, stride=8)
            spread[at, :] += lines[8 * r : 8 * r + 8, :]
    up = add_all([q_recv[flow_index[a, b, 1]] for a in (-1, 0, 1) for b in (-1, 0, 1)])
    down = add_all([q_recv[flow_index[a, b, -1]] for a in (-1, 0, 1) for b in (-1, 0, 1)])
    squares = blank
    for x in range(8):
        first = pltpu.roll(up, (128 - 16 * x - 8) % 128, 1)
        last = pltpu.roll(down, (123 - 16 * x) % 128, 1)
        tile = spread[pl.ds(8 * x, 8), :]
        tile = tile + jnp.where(lane < 5, first, jnp.where(lane >= 123, last, 0.0))
        spread[pl.ds(8 * x, 8), :] = tile
        squares = squares + tile * tile

    mine = gy * nz + gz
    ring_a[mine] = jnp.sum(squares, axis=0, keepdims=True)
    ring_copies = [send(ring_a.at[mine], ring_a.at[mine], move) for move in slab_moves]
    for copy in ring_copies:
        copy.wait_recv()
    ring_b[gx] = jnp.sum(ring_a[...], axis=0)
    ring_copies = [send(ring_b.at[gx], ring_b.at[gx], move) for move in line_moves]
    for copy in ring_copies:
        copy.wait_recv()
    total = jnp.sum(jnp.sum(ring_b[...], axis=0), axis=1, keepdims=True)
    mean_square = total / (8192.0 * nx * ny * nz)
    out_ref[...] = spread[pl.ds(0, 64), :] * lax.rsqrt(mean_square + norm_eps)
    rms_ref[...] = jnp.sqrt(mean_square)
    for copy in started:
        copy.wait_send()


def solution(mesh):
    sizes = tuple(mesh.shape[name] for name in ("gx", "gy", "gz"))
    table = lane_table()
    copies = 4 + 2 + 18 + 2 + 2 + 2 + 26 + (sizes[1] * sizes[2] - 1) + (sizes[0] - 1)

    def body(populations, design, flags, adjoint_seed):
        anywhere = pl.BlockSpec(memory_space=pl.ANY)
        inside = pl.BlockSpec(memory_space=pltpu.VMEM)
        scratch = [
            pltpu.VMEM((19, 64, 128), F32),
            pltpu.VMEM((64, 128), jnp.int32),
            pltpu.VMEM((8, 384), F32),
            pltpu.VMEM((19, 80, 128), F32),
            pltpu.VMEM((9, 80, 128), F32),
            pltpu.VMEM((19, 80, 128), F32),
            pltpu.VMEM((384, 128), F32),
            pltpu.VMEM((2, 15, 8, 128), F32),
            pltpu.VMEM((2, 15, 8, 128), F32),
            pltpu.VMEM((2, 40, 128), F32),
            pltpu.VMEM((2, 15, 8, 128), F32),
            pltpu.VMEM((2, 15, 24, 128), F32),
            pltpu.VMEM((4, 40, 128), F32),
            pltpu.VMEM((2, 2, 8, 128), F32),
            pltpu.VMEM((26, 2, 8, 128), F32),
            pltpu.VMEM((2, 8, 128), F32),
            pltpu.VMEM((256, 384), F32),
            pltpu.VMEM((256, 384), F32),
            pltpu.VMEM((384, 128), F32),
            pltpu.VMEM((384, 128), F32),
            pltpu.VMEM((9, 8, 128), F32),
            pltpu.VMEM((26, 8, 128), F32),
            pltpu.VMEM((sizes[1] * sizes[2], 1, 128), F32),
            pltpu.VMEM((sizes[0], 1, 128), F32),
            pltpu.VMEM((256, 384), BF16),
            pltpu.VMEM((256, 384), F32),
            pltpu.VMEM((384, 256), BF16),
            pltpu.VMEM((256, 128), BF16),
            pltpu.VMEM((256, 128), F32),
            pltpu.VMEM((32, 256), BF16),
            pltpu.VMEM((384, 256), BF16),
            pltpu.VMEM((384, 384), BF16),
            pltpu.VMEM((256, 256), F32),
            pltpu.VMEM((256, 128), F32),
            pltpu.SemaphoreType.DMA((5,)),
            pltpu.SemaphoreType.DMA((copies,)),
            pltpu.SemaphoreType.DMA((copies,)),
        ]
        grad, rms = pl.pallas_call(
            functools.partial(kernel, sizes),
            out_shape=(
                jax.ShapeDtypeStruct((64, 128), F32),
                jax.ShapeDtypeStruct((1, 1), F32),
            ),
            in_specs=[anywhere] * 5,
            out_specs=(inside, inside),
            scratch_shapes=scratch,
            compiler_params=pltpu.CompilerParams(
                collective_id=0, has_side_effects=True, vmem_limit_bytes=56 * 1024 * 1024
            ),
        )(
            populations.reshape(19, 64, 128),
            design.reshape(64, 128),
            flags.reshape(64, 128),
            adjoint_seed.reshape(19, 64, 128),
            jnp.asarray(table),
        )
        return grad.reshape(8, 8, 128), rms.reshape(())

    return jax.shard_map(
        body,
        mesh=mesh,
        in_specs=(
            P(None, "gx", "gy", "gz"),
            P("gx", "gy", "gz"),
            P("gx", "gy", "gz"),
            P(None, "gx", "gy", "gz"),
        ),
        out_specs=(P("gx", "gy", "gz"), P()),
        check_vma=False,
    )
```

time: 268 us -> 45.3 us (0.17)
  blocking collectives: 85 us -> 0 us
  starting transfers between devices: 62.2 us -> 0 us
  Pallas kernels: 0 us -> 41.3 us
  local copies, waits for them, and re-layouts: 41.5 us -> 1.38 us
  other arithmetic: 37.6 us -> 0 us
  waiting for transfers between devices: 36 us -> 0 us
    psum x1 -> x0, blocking collectives: 85 us -> none  [body(): squares = lax.psum(jnp.sum(raw_grad * raw_grad), ('gx', 'gy', 'gz'))]
    ppermute x30 -> x0, starting transfers between devices: 62.2 us -> none  [the longest x15 34.1 us: with_halo(): lax.ppermute(head, axis, [((i + 1) % count, i) for i in range(ends)])]
    pallas_call x0 -> x1, Pallas kernels: none -> 41.3 us  [body(): pl.pallas_call(functools.partial(kernel, sizes), out_shape=(jax.ShapeDtyp...]
    ppermute x30 -> x0, waiting for transfers between devices: 36 us -> none  [the longest x15 23.3 us: with_halo(): lax.ppermute(head, axis, [((i + 1) % count, i) for i in range(ends)])]
    unnamed x68 -> x0, other arithmetic: 22.9 us -> none
    slice x19 -> x0, local copies, waits for them, and re-layouts: 17.2 us -> none  [the longest x14 9.1 us: with_halo(): lax.slice_in_dim(cells, cells.shape[dim] - width, cells.shape[dim], axis=...]
    ppermute x6 -> x0, local copies, waits for them, and re-layouts: 14.4 us -> none  [the longest x3 7.72 us: with_halo(): lax.ppermute(tail, axis, [(i, (i + 1) % count) for i in range(ends)])]
    unnamed x170 -> x1, local copies, waits for them, and re-layouts: 9.06 us -> 1.38 us
  transfers between devices with their start and end apart: 30 -> 0, of which waited for: 16 -> 0; matrix products, arithmetic and copies ran while one was open for 9% -> 0% of each run, Pallas kernels for 0% -> 0%
where the time goes in v1:
time: 45.3 us; the launch traced here: 45.1 us
  Pallas kernels  41.3 us (91%)
  between operations  2.4 us (5%)
  local copies, waits for them, and re-layouts  1.38 us (3%)
    pallas_call x1, Pallas kernels, body(): pl.pallas_call(functools.partial(kernel, sizes), out_shape=(jax.ShapeDtyp...  41.3 us
    unnamed x1, local copies, waits for them, and re-layouts  1.38 us

profile of v1, /device:TPU:1, one launch (start us, length us, event | category | flops | bytes accessed | tf_op | source)
XLA Modules:
  0.0 45.1 jit_solution(14706625477919482240)
XLA Ops:
  0.6 41.3 %shard_map.68 = (f32[64,128]{1,0:T(8,128)}, f32[1,1]{1,0:T(1,128)}) custom-call(f32[19,64,128]{2,1,0:T(8,128)} %bitcast.6, f32[64,128]{1,0:T(8,128)} %bitcast.8, s32[64,128]{1,0:T(8,128)} %bitcast.9, f32[19,64,128]{2,1,0:T(8,128)} %bitcast.7, f32[8,384]{1,0:T(8,128)} %constant.2.clone.table_in), custom_call_target="tpu_custom_call" | custom-call | tf_op jit(solution)/shard_map/pallas_call | solution.py:749
  42.0 1.4 %copy.9 = f32[8,8,128]{2,1,0:T(8,128)} copy(f32[8,8,128]{2,1,0:T(8,128)} %bitcast.10) | data formatting | bytes 65536

commit v2 on v1

--- a/solution.py
+++ b/solution.py
@@ -2,7 +2,6 @@
 
 import jax
 import jax.numpy as jnp
-import numpy as np
 from jax import lax
 from jax.experimental import pallas as pl
 from jax.experimental.pallas import tpu as pltpu
@@ -53,7 +52,7 @@
 
 regions = {(0, 0): (0, 64)}
 for order, where_ in enumerate([(-1, 0), (1, 0), (0, -1), (0, 1), (-1, -1), (-1, 1), (1, -1), (1, 1)]):
-    regions[where_] = (64 + 40 * order, 40)
+    regions[where_] = (64 + 40 * order, 40) if order < 4 else (96 + 32 * order, 32)
 
 flows = [
     (a, b, c) for a in (1, -1, 0) for b in (1, -1, 0) for c in (1, -1, 0) if a or b or c
@@ -61,27 +60,22 @@
 flow_index = {flow: number for number, flow in enumerate(flows)}
 
 
-def lane_table():
-    table = np.zeros((8, 384), np.float32)
-    for (a, b), (start, rows) in regions.items():
-        for r in range(rows):
-            tile, sub = divmod(r, 8)
-            if (a, b) == (0, 0):
-                x, y = tile, sub
-            elif b == 0:
-                x, y = (tile - 5 if a < 0 else tile + 8), sub
-            else:
-                y = tile - 5 if b < 0 else tile + 8
-                x = sub + 8 * a
-            table[0, start + r] = x
-            table[1, start + r] = y
-    lanes = np.arange(384)
-    table[2] = np.where(lanes < 128, lanes, np.where(lanes < 256, lanes - 129, lanes - 255))
-    block = np.arange(256) // 16
-    table[3, :256] = np.where(block < 10, block - 1, 3 * FAR)
-    table[4, :256] = np.arange(256) % 16
-    table[5, :128] = np.where(np.arange(128) < 24, np.arange(128) - 8, 3 * FAR)
-    return table
+def outer_cells():
+    r = lax.broadcasted_iota(jnp.int32, (1, 384), 1)
+    low = jnp.bitwise_and(r, 7)
+    tile = lax.shift_right_logical(r, 3)
+    x = jnp.where(r < 64, tile, jnp.where(r < 104, tile - 13, jnp.where(r < 144, tile - 5, low)))
+    y = jnp.where(r < 144, low, jnp.where(r < 184, tile - 23, tile - 15))
+    k = jnp.bitwise_and(r, 31)
+    edge = lax.shift_right_logical(r, 5) - 7
+    part_y = lax.shift_right_logical(k * 13, 6)
+    part_x = k - 5 * part_y
+    edge_x = jnp.where(edge < 2, part_x - 5, part_x + 8)
+    edge_y = jnp.where(jnp.bitwise_and(edge, 1) == 0, part_y - 5, part_y + 8)
+    used = jnp.logical_and(k < 25, edge < 4)
+    x = jnp.where(r < 224, x, jnp.where(used, edge_x, 12288))
+    y = jnp.where(r < 224, y, jnp.where(used, edge_y, 12288))
+    return x.astype(F32), y.astype(F32)
 
 
 def split(value):
@@ -256,12 +250,10 @@
     design_in,
     flags_in,
     seed_in,
-    table_in,
     out_ref,
     rms_ref,
     pops,
     flags_v,
-    table,
     first_v,
     slope_v,
     seed_v,
@@ -272,6 +264,7 @@
     y_send,
     y_rows,
     xy_send,
+    mixed_send,
     z_send,
     z_recv,
     z_pack,
@@ -324,7 +317,6 @@
         pl.semaphore_signal(barrier, inc=1, device_id=device(move), device_id_type=MESH)
 
     loads = [
-        pltpu.make_async_copy(table_in, table, local_sem.at[0]),
         pltpu.make_async_copy(pop_in, pops, local_sem.at[1]),
         pltpu.make_async_copy(flags_in, flags_v, local_sem.at[2]),
         pltpu.make_async_copy(seed_in, seed_v.at[:, pl.ds(8, 64), :], local_sem.at[3]),
@@ -398,13 +390,81 @@
             y_field[n, pl.ds(8 * r, 8), :] = field[
                 pl.ds(3 + r if sign == 1 else r, 8, stride=8), :
             ]
+    packs = {1: pack_up, -1: pack_down}
+    mixed = [flow for flow in flows if flow[2] and (flow[0] == 0) != (flow[1] == 0)]
+    for n, (a, b, c) in enumerate(mixed):
+        if a:
+            s = crossing[2, c].index(velocities.index((a, b, c)))
+            tile = quad
+            for k in range(3):
+                free = k if a == 1 else 112 + k
+                place = 40 * k + 8 * s + (7 if a == 1 else 0)
+                tile = jnp.where(
+                    lane == free, pltpu.roll(packs[c], (free - place) % 128, 1), tile
+                )
+        elif b == 1:
+            tile = jnp.where(row == 0, pltpu.roll(packs[c], 1, 0), quad)
+        else:
+            tile = jnp.where(row == 7, pltpu.roll(packs[c], 7, 0), quad)
+        mixed_send[n] = tile
     diagonals = [(a, b) for a in (1, -1) for b in (1, -1)]
     for n, (a, b) in enumerate(diagonals):
         j = velocities.index((a, b, 0))
-        xy_send[n] = y_field[side[b]]
+        for r in range(5):
+            at = (24 if a == 1 else 0) + (3 + r if b == 1 else r)
+            xy_send[n, pl.ds(5 * r, 5), :] = field[pl.ds(at, 5, stride=8), :]
         for k in range(3):
             at = (8 if a == 1 else 1) * 8 + (7 if b == 1 else 0)
-            xy_send[n, pl.ds(k if a == 1 else 5 + k, 1), :] = own(k, j, pl.ds(at, 1))
+            xy_send[n, pl.ds(25 + k, 1), :] = own(k, j, pl.ds(at, 1))
+        xy_send[n, pl.ds(28, 4), :] = jnp.zeros((4, 128), F32)
+
+    pl.semaphore_wait(barrier, len(partners))
+    count = [0]
+    started = []
+
+    def send(source, target, move):
+        n = count[0]
+        count[0] += 1
+        copy = pltpu.make_async_remote_copy(
+            src_ref=source,
+            dst_ref=target,
+            send_sem=send_sem.at[n],
+            recv_sem=recv_sem.at[n],
+            device_id=device(move),
+            device_id_type=MESH,
+        )
+        copy.start()
+        started.append(copy)
+        return copy
+
+    def region(a, b):
+        start, rows = regions[a, b]
+        return pl.ds(start, rows)
+
+    field_copies, fill_copies = [], []
+    for n, (a, b) in enumerate(diagonals):
+        field_copies.append(send(xy_send.at[n], field.at[region(-a, -b)], (a, b, 0)))
+    for a in (1, -1):
+        source = pl.ds(24, 40) if a == 1 else pl.ds(0, 40)
+        field_copies.append(send(field.at[source], field.at[region(-a, 0)], (a, 0, 0)))
+    for flow in flows:
+        if flow[2] != 0:
+            n = flow_index[flow]
+            if flow[0] != 0 and flow[1] != 0:
+                source, target = z_send.at[side[flow[2]], 0], z_recv.at[n, 0]
+            elif flow in mixed:
+                source, target = mixed_send.at[mixed.index(flow)], z_recv.at[n, 0]
+            else:
+                source, target = z_send.at[side[flow[2]]], z_recv.at[n]
+            field_copies.append(send(source, target, flow))
+    for b in (1, -1):
+        field_copies.append(send(y_field.at[side[b]], field.at[region(0, -b)], (0, b, 0)))
+    for a in (1, -1):
+        fill_copies.append(send(x_send.at[side[a]], x_recv.at[side[a]], (a, 0, 0)))
+    for b in (1, -1):
+        fill_copies.append(
+            send(y_send.at[side[b]], y_rows.at[side[b], :, pl.ds(8, 8), :], (0, b, 0))
+        )
 
     def one_if(condition):
         return jnp.where(condition, 1.0, 0.0).astype(F32)
@@ -412,15 +472,19 @@
     x_low, x_high = one_if(gx == 0), one_if(gx == nx - 1)
     y_low, y_high = one_if(gy == 0), one_if(gy == ny - 1)
     z_low, z_high = one_if(gz == 0), one_if(gz == nz - 1)
-    lanes_x = cut(table[0:1, :], 7.0, x_low, x_high)
-    lanes_y = cut(table[1:2, :], 7.0, y_low, y_high)
-    lanes_z = cut(table[2:3, :], 127.0, z_low, z_high)
-    blocks_x = cut(table[3:4, 0:256], 7.0, x_low, x_high)
-    blocks_part = table[4:5, 0:256]
-    stack_y = cut(table[5:6, 0:128], 7.0, y_low, y_high)
-    lane_scale = 1.0 / weight_total(
-        table[2:3, :] + (gz * 128).astype(F32), 128.0 * nz
-    )
+    lanes_x, lanes_y = outer_cells()
+    lanes_x = cut(lanes_x, 7.0, x_low, x_high)
+    lanes_y = cut(lanes_y, 7.0, y_low, y_high)
+    wide = lax.broadcasted_iota(jnp.int32, (1, 384), 1)
+    plain_z = jnp.where(wide < 128, wide, jnp.where(wide < 256, wide - 129, wide - 255)).astype(F32)
+    lanes_z = cut(plain_z, 127.0, z_low, z_high)
+    line = lax.broadcasted_iota(jnp.int32, (1, 128), 1)
+    tenth = lax.shift_right_logical(line * 205, 11)
+    part_ten = line - 10 * tenth
+    blocks_x = cut(jnp.where(tenth < 10, tenth - 1, 12288).astype(F32), 7.0, x_low, x_high)
+    blocks_part = jnp.where(part_ten < 5, part_ten, part_ten + 3)
+    stack_y = cut(jnp.where(line < 24, line - 8, 12288).astype(F32), 7.0, y_low, y_high)
+    lane_scale = 1.0 / weight_total(plain_z + (gz * 128).astype(F32), 128.0 * nz)
 
     def build_rows(t, carry):
         rows = pl.ds(pl.multiple_of(t * 16, 16), 16)
@@ -444,10 +508,7 @@
         repeated = hat(cut_y - stack_y)
         rep_l_wide[rows, :] = repeated
         rep_l[rows, :] = repeated.astype(BF16)
-        block = lax.shift_right_logical(lax.broadcasted_iota(jnp.int32, (16, 256), 1), 4)
-        block_mask[rows, :] = jnp.where(
-            block == jnp.concatenate([plane] * 2, axis=1), 1.0, 0.0
-        )
+        block_mask[rows, :] = jnp.where(tenth == plane, 1.0, 0.0)
         return carry
 
     lax.fori_loop(0, 16, build_rows, 0)
@@ -457,7 +518,7 @@
     def build_cross(t, carry):
         rows = pl.ds(pl.multiple_of(t * 16, 16), 16)
         x = cut((t - 8).astype(F32), 7.0, x_low, x_high)
-        same = lax.broadcasted_iota(jnp.int32, (16, 256), 0).astype(F32) == blocks_part
+        same = lax.broadcasted_iota(jnp.int32, (16, 128), 0) == blocks_part
         cross_x[rows, :] = jnp.where(same, hat(x - blocks_x), 0.0).astype(BF16)
         return carry
 
@@ -465,65 +526,16 @@
 
     def build_z(t, carry):
         rows = pl.ds(pl.multiple_of(t * 16, 16), 16)
-        index = lax.broadcasted_iota(jnp.int32, (16, 384), 0)
-        inside = index + t * 16
-        halo = jnp.where(
-            index < 5,
-            index - 5,
-            jnp.where(jnp.logical_and(index >= 8, index < 13), index + 120, 100000),
-        )
-        z = cut(jnp.where(t < 8, inside, halo).astype(F32), 127.0, z_low, z_high)
+        index = lax.broadcasted_iota(jnp.int32, (16, 384), 0) + t * 16
+        halo = index - 128
+        halo = halo - 10 * lax.shift_right_logical(halo * 205, 11)
+        halo = jnp.where(halo < 5, halo - 5, halo + 123)
+        z = cut(jnp.where(index < 128, index, halo).astype(F32), 127.0, z_low, z_high)
         cross_z[rows, :] = hat(z - lanes_z).astype(BF16)
         return carry
 
-    lax.fori_loop(0, 24, build_z, 0)
+    lax.fori_loop(0, 16, build_z, 0)
     grad_v[...] = jnp.zeros_like(grad_v)
-
-    pl.semaphore_wait(barrier, len(partners))
-    count = [0]
-    started = []
-
-    def send(source, target, move):
-        n = count[0]
-        count[0] += 1
-        copy = pltpu.make_async_remote_copy(
-            src_ref=source,
-            dst_ref=target,
-            send_sem=send_sem.at[n],
-            recv_sem=recv_sem.at[n],
-            device_id=device(move),
-            device_id_type=MESH,
-        )
-        copy.start()
-        started.append(copy)
-        return copy
-
-    def region(a, b):
-        start, rows = regions[a, b]
-        return pl.ds(start, rows)
-
-    field_copies, fill_copies = [], []
-    for n, (a, b) in enumerate(diagonals):
-        field_copies.append(send(xy_send.at[n], field.at[region(-a, -b)], (a, b, 0)))
-    for a in (1, -1):
-        source = pl.ds(24, 40) if a == 1 else pl.ds(0, 40)
-        field_copies.append(send(field.at[source], field.at[region(-a, 0)], (a, 0, 0)))
-    for flow in flows:
-        if flow[2] != 0:
-            n = flow_index[flow]
-            if flow[0] != 0 and flow[1] != 0:
-                source, target = z_send.at[side[flow[2]], 0], z_recv.at[n, 0]
-            else:
-                source, target = z_send.at[side[flow[2]]], z_recv.at[n]
-            field_copies.append(send(source, target, flow))
-    for b in (1, -1):
-        field_copies.append(send(y_field.at[side[b]], field.at[region(0, -b)], (0, b, 0)))
-    for a in (1, -1):
-        fill_copies.append(send(x_send.at[side[a]], x_recv.at[side[a]], (a, 0, 0)))
-    for b in (1, -1):
-        fill_copies.append(
-            send(y_send.at[side[b]], y_rows.at[side[b], :, pl.ds(8, 8), :], (0, b, 0))
-        )
 
     for copy in field_copies:
         copy.wait_recv()
@@ -539,7 +551,7 @@
         stacked.append(jnp.concatenate(tiles, axis=1))
     stacked.append(jnp.zeros((8, 384), F32))
     halo_x = right_dot(jnp.concatenate(stacked, axis=0), cross_x[...])
-    halo_x = jnp.concatenate([halo_x, jnp.zeros((96, 256), F32)], axis=0)
+    halo_x = jnp.concatenate([halo_x, jnp.zeros((96, 128), F32)], axis=0)
     halo_xy = left_dot(rep_l[...], halo_x) * block_mask[...]
     summed = right_dot(jnp.concatenate([inner_xy, halo_xy], axis=1), cross_z[...])
     scale_rows = jnp.concatenate([row_scale[...]] * 3, axis=1)
@@ -560,28 +572,27 @@
         start = regions[-a, -b][0]
         for k in range(3):
             y_rows[side[b], 5 * k + s, pl.ds(7 if a == 1 else 16, 1), :] = field[
-                pl.ds(start + (k if a == 1 else 5 + k), 1), :
+                pl.ds(start + 25 + k, 1), :
             ]
     eighth = lax.shift_right_logical(lane, 3)
     slot = eighth - jnp.where(eighth >= 10, 10, jnp.where(eighth >= 5, 5, 0))
-    step = jnp.bitwise_and(lane, 7)
     for sign in (1, -1):
         base = z_recv[flow_index[0, 0, sign], 1]
         total = base
         for s, j in enumerate(crossing[2, sign]):
             a, b, _ = velocities[j]
             if a != 0:
-                corner = z_recv[flow_index[a, 0, sign], 1]
-                if a == 1:
-                    moved = jnp.where(step == 0, pltpu.roll(corner, 121, 1), pltpu.roll(base, 1, 1))
-                else:
-                    moved = jnp.where(step == 7, pltpu.roll(corner, 7, 1), pltpu.roll(base, 127, 1))
+                corner = z_recv[flow_index[a, 0, sign], 0]
+                moved = pltpu.roll(base, a % 128, 1)
+                for k in range(3):
+                    free = k if a == 1 else 112 + k
+                    place = 40 * k + 8 * s + (0 if a == 1 else 7)
+                    moved = jnp.where(
+                        lane == place, pltpu.roll(corner, (place - free) % 128, 1), moved
+                    )
             elif b != 0:
-                corner = z_recv[flow_index[0, b, sign], 1]
-                if b == 1:
-                    moved = pltpu.roll(jnp.where(row == 7, corner, base), 1, 0)
-                else:
-                    moved = pltpu.roll(jnp.where(row == 0, corner, base), 7, 0)
+                corner = z_recv[flow_index[0, b, sign], 0]
+                moved = jnp.where(row == (0 if b == 1 else 7), corner, pltpu.roll(base, b % 8, 0))
             else:
                 continue
             total = jnp.where(slot == s, moved, total)
@@ -642,7 +653,7 @@
     scaled = grad_v[...] * (scale_rows * (-0.5 * lane_scale))
     summed = right_dot_t(scaled, cross_z[...])
     spread[...] = left_dot(big_lt[...], summed[:, 0:128])
-    halo_x = left_dot(rep_lt[...], summed[:, 128:384] * block_mask[...])
+    halo_x = left_dot(rep_lt[...], summed[:, 128:256] * block_mask[...])
     halo = right_dot_t(halo_x, cross_x[...])
     for b in range(3):
         for a in range(3):
@@ -663,14 +674,15 @@
     spread[pl.ds(24, 40), :] += spread_recv[region(-1, 0), :]
     spread[pl.ds(0, 40), :] += spread_recv[region(1, 0), :]
     for b in (1, -1):
-        lines = (
-            spread_recv[region(0, b), :]
-            + spread_recv[region(-1, b), :]
-            + spread_recv[region(1, b), :]
-        )
         for r in range(5):
-            at = pl.ds(r if b == 1 else 3 + r, 8, stride=8)
-            spread[at, :] += lines[8 * r : 8 * r + 8, :]
+            y = r if b == 1 else 3 + r
+            spread[pl.ds(y, 8, stride=8), :] += spread_recv[
+                pl.ds(regions[0, b][0] + 8 * r, 8), :
+            ]
+            for a in (1, -1):
+                spread[pl.ds(y + (0 if a == 1 else 24), 5, stride=8), :] += spread_recv[
+                    pl.ds(regions[a, b][0] + 5 * r, 5), :
+                ]
     up = add_all([q_recv[flow_index[a, b, 1]] for a in (-1, 0, 1) for b in (-1, 0, 1)])
     down = add_all([q_recv[flow_index[a, b, -1]] for a in (-1, 0, 1) for b in (-1, 0, 1)])
     squares = blank
@@ -701,7 +713,6 @@
 
 def solution(mesh):
     sizes = tuple(mesh.shape[name] for name in ("gx", "gy", "gz"))
-    table = lane_table()
     copies = 4 + 2 + 18 + 2 + 2 + 2 + 26 + (sizes[1] * sizes[2] - 1) + (sizes[0] - 1)
 
     def body(populations, design, flags, adjoint_seed):
@@ -710,7 +721,6 @@
         scratch = [
             pltpu.VMEM((19, 64, 128), F32),
             pltpu.VMEM((64, 128), jnp.int32),
-            pltpu.VMEM((8, 384), F32),
             pltpu.VMEM((19, 80, 128), F32),
             pltpu.VMEM((9, 80, 128), F32),
             pltpu.VMEM((19, 80, 128), F32),
@@ -720,7 +730,8 @@
             pltpu.VMEM((2, 40, 128), F32),
             pltpu.VMEM((2, 15, 8, 128), F32),
             pltpu.VMEM((2, 15, 24, 128), F32),
-            pltpu.VMEM((4, 40, 128), F32),
+            pltpu.VMEM((4, 32, 128), F32),
+            pltpu.VMEM((8, 8, 128), F32),
             pltpu.VMEM((2, 2, 8, 128), F32),
             pltpu.VMEM((26, 2, 8, 128), F32),
             pltpu.VMEM((2, 8, 128), F32),
@@ -738,9 +749,9 @@
             pltpu.VMEM((256, 128), BF16),
             pltpu.VMEM((256, 128), F32),
             pltpu.VMEM((32, 256), BF16),
-            pltpu.VMEM((384, 256), BF16),
-            pltpu.VMEM((384, 384), BF16),
-            pltpu.VMEM((256, 256), F32),
+            pltpu.VMEM((384, 128), BF16),
+            pltpu.VMEM((256, 384), BF16),
+            pltpu.VMEM((256, 128), F32),
             pltpu.VMEM((256, 128), F32),
             pltpu.SemaphoreType.DMA((5,)),
             pltpu.SemaphoreType.DMA((copies,)),
@@ -752,18 +763,17 @@
                 jax.ShapeDtypeStruct((64, 128), F32),
                 jax.ShapeDtypeStruct((1, 1), F32),
             ),
-            in_specs=[anywhere] * 5,
+            in_specs=[anywhere] * 4,
             out_specs=(inside, inside),
             scratch_shapes=scratch,
             compiler_params=pltpu.CompilerParams(
-                collective_id=0, has_side_effects=True, vmem_limit_bytes=56 * 1024 * 1024
+                collective_id=0, has_side_effects=True, vmem_limit_bytes=56491008
             ),
         )(
             populations.reshape(19, 64, 128),
             design.reshape(64, 128),
             flags.reshape(64, 128),
             adjoint_seed.reshape(19, 64, 128),
-            jnp.asarray(table),
         )
         return grad.reshape(8, 8, 128), rms.reshape(())
 

time: 45.3 us -> 42.4 us (0.936)
  Pallas kernels: 41.3 us -> 39.3 us
  local copies, waits for them, and re-layouts: 1.38 us -> 0.62 us
    pallas_call x1, Pallas kernels: 41.3 us -> 39.3 us  [body(): pl.pallas_call(functools.partial(kernel, sizes), out_shape=(jax.ShapeDtyp...]
    unnamed x1, local copies, waits for them, and re-layouts: 1.38 us -> 0.62 us
where the time goes in v2:
time: 42.4 us; the launch traced here: 42.3 us
  Pallas kernels  39.3 us (93%)
  between operations  2.33 us (5%)
  local copies, waits for them, and re-layouts  0.62 us (1%)
    pallas_call x1, Pallas kernels, body(): pl.pallas_call(functools.partial(kernel, sizes), out_shape=(jax.ShapeDtyp...  39.3 us

profile of v2, /device:TPU:1, one launch (start us, length us, event | category | flops | bytes accessed | tf_op | source)
XLA Modules:
  0.0 42.3 jit_solution(18135042210122856783)
XLA Ops:
  0.6 39.3 %shard_map.59 = (f32[64,128]{1,0:T(8,128)S(1)}, f32[1,1]{1,0:T(1,128)}) custom-call(f32[19,64,128]{2,1,0:T(8,128)} %bitcast.7, f32[64,128]{1,0:T(8,128)} %bitcast.9, s32[64,128]{1,0:T(8,128)} %bitcast.10, f32[19,64,128]{2,1,0:T(8,128)} %bitcast.8), custom_call_target="tpu_custom_call" | custom-call | tf_op jit(solution)/shard_map/pallas_call | solution.py:760
  40.0 0.6 %copy.8 = f32[8,8,128]{2,1,0:T(8,128)} copy(f32[8,8,128]{2,1,0:T(8,128)S(1)} %bitcast.6) | data formatting | bytes 65536

commit v3 on v2

--- a/solution.py
+++ b/solution.py
@@ -84,10 +84,11 @@
 
 
 def left_dot(matrix, value):
-    high, low = split(value)
-    return jnp.dot(matrix, high, preferred_element_type=F32) + jnp.dot(
-        matrix, low, preferred_element_type=F32
+    both = jnp.dot(
+        matrix, jnp.concatenate(split(value), axis=1), preferred_element_type=F32
     )
+    width = value.shape[1]
+    return both[:, :width] + both[:, width:]
 
 
 def right_dot(value, matrix):
@@ -293,12 +294,15 @@
     nx, ny, nz = sizes
     gx, gy, gz = lax.axis_index("gx"), lax.axis_index("gy"), lax.axis_index("gz")
 
+    def around(start, length):
+        if length & (length - 1) == 0:
+            return [jnp.bitwise_and(start + n, length - 1) for n in range(length)]
+        return [lax.rem(start + n, length) for n in range(length)]
+
+    place_x, place_y, place_z = around(gx, nx), around(gy, ny), around(gz, nz)
+
     def device(move):
-        return (
-            lax.rem(gx + move[0] % nx, nx),
-            lax.rem(gy + move[1] % ny, ny),
-            lax.rem(gz + move[2] % nz, nz),
-        )
+        return place_x[move[0] % nx], place_y[move[1] % ny], place_z[move[2] % nz]
 
     slab_moves = [(0, b, c) for b in range(ny) for c in range(nz) if b or c]
     slab_moves.sort(key=lambda m: -(min(m[1], ny - m[1]) + min(m[2], nz - m[2])))
@@ -373,7 +377,7 @@
         return packs[0], packs[1], quad
 
     blank = jnp.zeros((8, 128), F32)
-    pack_up, pack_down, quad = lax.fori_loop(0, 8, start_step, (blank, blank, blank))
+    pack_up, pack_down, quad = lax.fori_loop(0, 8, start_step, (blank, blank, blank), unroll=2)
     z_send[0, 0] = quad
     z_send[1, 0] = quad
     z_send[0, 1] = pack_up
@@ -557,23 +561,8 @@
     scale_rows = jnp.concatenate([row_scale[...]] * 3, axis=1)
     kappa_v[...] = 0.5 * (1.0 - summed * scale_rows * lane_scale)
 
-    for copy in fill_copies:
+    for copy in fill_copies[2:]:
         copy.wait_recv()
-    for sign in (1, -1):
-        n = side[sign]
-        rows = pl.ds(0, 8) if sign == 1 else pl.ds(72, 8)
-        for s, j in enumerate(crossing[0, sign]):
-            first_v[j, rows, :] = x_recv[n, s]
-            slope_v[(j - 1) // 2, rows, :] = x_recv[n, 5 + s]
-            seed_v[opposite[j], rows, :] = x_recv[n, 10 + s]
-    for a, b in diagonals:
-        j = velocities.index((a, b, 0))
-        s = crossing[1, b].index(j)
-        start = regions[-a, -b][0]
-        for k in range(3):
-            y_rows[side[b], 5 * k + s, pl.ds(7 if a == 1 else 16, 1), :] = field[
-                pl.ds(start + 25 + k, 1), :
-            ]
     eighth = lax.shift_right_logical(lane, 3)
     slot = eighth - jnp.where(eighth >= 10, 10, jnp.where(eighth >= 5, 5, 0))
     for sign in (1, -1):
@@ -648,7 +637,25 @@
                 grad_v[rows, lanes] -= slopes[j] * back[j]
         return carry
 
-    lax.fori_loop(0, 8, plane_step, 0)
+    lax.fori_loop(1, 7, plane_step, 0, unroll=6)
+    for copy in fill_copies[:2]:
+        copy.wait_recv()
+    for sign in (1, -1):
+        n = side[sign]
+        rows = pl.ds(0, 8) if sign == 1 else pl.ds(72, 8)
+        for s, j in enumerate(crossing[0, sign]):
+            first_v[j, rows, :] = x_recv[n, s]
+            slope_v[(j - 1) // 2, rows, :] = x_recv[n, 5 + s]
+            seed_v[opposite[j], rows, :] = x_recv[n, 10 + s]
+    for a, b in diagonals:
+        j = velocities.index((a, b, 0))
+        s = crossing[1, b].index(j)
+        start = regions[-a, -b][0]
+        for k in range(3):
+            y_rows[side[b], 5 * k + s, pl.ds(7 if a == 1 else 16, 1), :] = field[
+                pl.ds(start + 25 + k, 1), :
+            ]
+    lax.fori_loop(0, 2, lambda n, carry: plane_step(7 * n, carry), 0, unroll=2)
 
     scaled = grad_v[...] * (scale_rows * (-0.5 * lane_scale))
     summed = right_dot_t(scaled, cross_z[...])
@@ -705,8 +712,8 @@
         copy.wait_recv()
     total = jnp.sum(jnp.sum(ring_b[...], axis=0), axis=1, keepdims=True)
     mean_square = total / (8192.0 * nx * ny * nz)
-    out_ref[...] = spread[pl.ds(0, 64), :] * lax.rsqrt(mean_square + norm_eps)
-    rms_ref[...] = jnp.sqrt(mean_square)
+    out_ref[...] = spread[pl.ds(0, 64), :]
+    rms_ref[...] = jnp.broadcast_to(jnp.sqrt(mean_square), (64, 128))
     for copy in started:
         copy.wait_send()
 
@@ -761,13 +768,13 @@
             functools.partial(kernel, sizes),
             out_shape=(
                 jax.ShapeDtypeStruct((64, 128), F32),
-                jax.ShapeDtypeStruct((1, 1), F32),
+                jax.ShapeDtypeStruct((64, 128), F32),
             ),
             in_specs=[anywhere] * 4,
             out_specs=(inside, inside),
             scratch_shapes=scratch,
             compiler_params=pltpu.CompilerParams(
-                collective_id=0, has_side_effects=True, vmem_limit_bytes=56491008
+                collective_id=0, has_side_effects=True, vmem_limit_bytes=56470528
             ),
         )(
             populations.reshape(19, 64, 128),
@@ -775,7 +782,7 @@
             flags.reshape(64, 128),
             adjoint_seed.reshape(19, 64, 128),
         )
-        return grad.reshape(8, 8, 128), rms.reshape(())
+        return grad.reshape(8, 8, 128) * lax.rsqrt(rms.reshape(8, 8, 128) * rms.reshape(8, 8, 128) + norm_eps), jnp.max(rms.reshape(8, 8, 128))
 
     return jax.shard_map(
         body,

time: 42.4 us -> 39.4 us (0.929)
  Pallas kernels: 39.3 us -> 37.4 us
  between operations: 2.33 us -> 0.64 us
  other arithmetic: 0 us -> 1.23 us
  local copies, waits for them, and re-layouts: 0.62 us -> 0 us
    pallas_call x1, Pallas kernels: 39.3 us -> 37.4 us  [body(): pl.pallas_call(functools.partial(kernel, sizes), out_shape=(jax.ShapeDtyp...]
    reduce_max x0 -> x1, other arithmetic: none -> 1.23 us  [body(): jnp.max(rms.reshape(8, 8, 128))]
    unnamed x1 -> x0, local copies, waits for them, and re-layouts: 0.62 us -> none
where the time goes in v3:
time: 39.4 us; the launch traced here: 39.3 us
  Pallas kernels  37.4 us (95%)
  other arithmetic  1.23 us (3%)
  between operations  0.64 us (2%)
    pallas_call x1, Pallas kernels, body(): pl.pallas_call(functools.partial(kernel, sizes), out_shape=(jax.ShapeDtyp...  37.4 us
    reduce_max x1, other arithmetic, body(): jnp.max(rms.reshape(8, 8, 128))  1.23 us

profile of v3, /device:TPU:1, one launch (start us, length us, event | category | flops | bytes accessed | tf_op | source)
XLA Modules:
  0.0 39.3 jit_solution(1306045826637001730)
XLA Ops:
  0.6 37.4 %shard_map.59 = (f32[64,128]{1,0:T(8,128)S(1)}, f32[64,128]{1,0:T(8,128)S(1)}) custom-call(f32[19,64,128]{2,1,0:T(8,128)} %bitcast.6, f32[64,128]{1,0:T(8,128)} %bitcast.8, s32[64,128]{1,0:T(8,128)} %bitcast.9, f32[19,64,128]{2,1,0:T(8,128)} %bitcast.7), custom_call_target="tpu_custom_call" | custom-call | tf_op jit(solution)/shard_map/pallas_call | solution.py:767
  38.0 1.2 %fusion = (f32[]{:T(128)}, f32[8,8,128]{2,1,0:T(8,128)}) fusion(f32[64,128]{1,0:T(8,128)S(1)} %get-tuple-element.5, f32[64,128]{1,0:T(8,128)S(1)} %get-tuple-element.4), kind=kLoop, calls=%fused_computation.1 | loop fusion | flops 32767 | bytes 98308 | tf_op jit(solution)/shard_map/reduce_max | solution.py:785

commit v4 on v3

--- a/solution.py
+++ b/solution.py
@@ -285,6 +285,10 @@
     rep_lt,
     cross_x,
     cross_z,
+    cross_xt,
+    cross_zt,
+    wide_x_v,
+    wide_z_v,
     block_mask,
     row_scale,
     local_sem,
@@ -523,7 +527,9 @@
         rows = pl.ds(pl.multiple_of(t * 16, 16), 16)
         x = cut((t - 8).astype(F32), 7.0, x_low, x_high)
         same = lax.broadcasted_iota(jnp.int32, (16, 128), 0) == blocks_part
-        cross_x[rows, :] = jnp.where(same, hat(x - blocks_x), 0.0).astype(BF16)
+        weights = jnp.where(same, hat(x - blocks_x), 0.0)
+        wide_x_v[rows, :] = weights
+        cross_x[rows, :] = weights.astype(BF16)
         return carry
 
     lax.fori_loop(0, 24, build_cross, 0)
@@ -535,15 +541,21 @@
         halo = halo - 10 * lax.shift_right_logical(halo * 205, 11)
         halo = jnp.where(halo < 5, halo - 5, halo + 123)
         z = cut(jnp.where(index < 128, index, halo).astype(F32), 127.0, z_low, z_high)
-        cross_z[rows, :] = hat(z - lanes_z).astype(BF16)
+        weights = hat(z - lanes_z)
+        wide_z_v[rows, :] = weights
+        cross_z[rows, :] = weights.astype(BF16)
         return carry
 
     lax.fori_loop(0, 16, build_z, 0)
+    cross_xt[...] = wide_x_v[...].T.astype(BF16)
+    cross_zt[...] = wide_z_v[...].T.astype(BF16)
     grad_v[...] = jnp.zeros_like(grad_v)
 
-    for copy in field_copies:
+    for copy in field_copies[:6] + field_copies[-2:]:
         copy.wait_recv()
     inner_xy = left_dot(big_l[...], field[...])
+    for copy in field_copies[6:-2]:
+        copy.wait_recv()
     part = jnp.bitwise_and(lane, 15)
     stacked = []
     for b in (-1, 0, 1):
@@ -658,13 +670,8 @@
     lax.fori_loop(0, 2, lambda n, carry: plane_step(7 * n, carry), 0, unroll=2)
 
     scaled = grad_v[...] * (scale_rows * (-0.5 * lane_scale))
-    summed = right_dot_t(scaled, cross_z[...])
+    summed = right_dot(scaled, cross_zt[...])
     spread[...] = left_dot(big_lt[...], summed[:, 0:128])
-    halo_x = left_dot(rep_lt[...], summed[:, 128:256] * block_mask[...])
-    halo = right_dot_t(halo_x, cross_x[...])
-    for b in range(3):
-        for a in range(3):
-            q_out[3 * b + a] = halo[8 * b : 8 * b + 8, 128 * a : 128 * a + 128]
     spread_copies = []
     for flow in flows:
         a, b, c = flow
@@ -672,50 +679,73 @@
             spread_copies.append(
                 send(spread.at[region(a, b)], spread_recv.at[region(a, b)], flow)
             )
-        else:
+    halo_x = left_dot(rep_lt[...], summed[:, 128:256] * block_mask[...])
+    halo = right_dot(halo_x, cross_xt[...])
+    for b in range(3):
+        for a in range(3):
+            q_out[3 * b + a] = halo[8 * b : 8 * b + 8, 128 * a : 128 * a + 128]
+    for flow in flows:
+        a, b, c = flow
+        if c != 0:
             spread_copies.append(
                 send(q_out.at[3 * (b + 1) + a + 1], q_recv.at[flow_index[flow]], flow)
             )
-    for copy in spread_copies:
-        copy.wait_recv()
-    spread[pl.ds(24, 40), :] += spread_recv[region(-1, 0), :]
-    spread[pl.ds(0, 40), :] += spread_recv[region(1, 0), :]
+    arrived = dict(zip([f for f in flows if f[2] == 0] + [f for f in flows if f[2] != 0], spread_copies))
     for b in (1, -1):
+        arrived[0, b, 0].wait_recv()
         for r in range(5):
             y = r if b == 1 else 3 + r
             spread[pl.ds(y, 8, stride=8), :] += spread_recv[
                 pl.ds(regions[0, b][0] + 8 * r, 8), :
             ]
-            for a in (1, -1):
-                spread[pl.ds(y + (0 if a == 1 else 24), 5, stride=8), :] += spread_recv[
-                    pl.ds(regions[a, b][0] + 5 * r, 5), :
-                ]
+    for flow in reversed(flows):
+        if flow[2] != 0:
+            arrived[flow].wait_recv()
     up = add_all([q_recv[flow_index[a, b, 1]] for a in (-1, 0, 1) for b in (-1, 0, 1)])
     down = add_all([q_recv[flow_index[a, b, -1]] for a in (-1, 0, 1) for b in (-1, 0, 1)])
-    squares = blank
     for x in range(8):
         first = pltpu.roll(up, (128 - 16 * x - 8) % 128, 1)
         last = pltpu.roll(down, (123 - 16 * x) % 128, 1)
+        spread[pl.ds(8 * x, 8), :] += jnp.where(
+            lane < 5, first, jnp.where(lane >= 123, last, 0.0)
+        )
+    arrived[-1, 0, 0].wait_recv()
+    spread[pl.ds(24, 40), :] += spread_recv[region(-1, 0), :]
+    arrived[1, 0, 0].wait_recv()
+    spread[pl.ds(0, 40), :] += spread_recv[region(1, 0), :]
+    for a, b in diagonals:
+        arrived[a, b, 0].wait_recv()
+        for r in range(5):
+            y = r if b == 1 else 3 + r
+            spread[pl.ds(y + (0 if a == 1 else 24), 5, stride=8), :] += spread_recv[
+                pl.ds(regions[a, b][0] + 5 * r, 5), :
+            ]
+    squares = blank
+    for x in range(8):
         tile = spread[pl.ds(8 * x, 8), :]
-        tile = tile + jnp.where(lane < 5, first, jnp.where(lane >= 123, last, 0.0))
-        spread[pl.ds(8 * x, 8), :] = tile
         squares = squares + tile * tile
 
     mine = gy * nz + gz
     ring_a[mine] = jnp.sum(squares, axis=0, keepdims=True)
     ring_copies = [send(ring_a.at[mine], ring_a.at[mine], move) for move in slab_moves]
-    for copy in ring_copies:
+    for copy in reversed(ring_copies):
         copy.wait_recv()
     ring_b[gx] = jnp.sum(ring_a[...], axis=0)
     ring_copies = [send(ring_b.at[gx], ring_b.at[gx], move) for move in line_moves]
-    for copy in ring_copies:
+    for copy in reversed(ring_copies):
         copy.wait_recv()
     total = jnp.sum(jnp.sum(ring_b[...], axis=0), axis=1, keepdims=True)
     mean_square = total / (8192.0 * nx * ny * nz)
     out_ref[...] = spread[pl.ds(0, 64), :]
-    rms_ref[...] = jnp.broadcast_to(jnp.sqrt(mean_square), (64, 128))
+    rms_ref[...] = jnp.broadcast_to(mean_square, (8, 128))
     for copy in started:
         copy.wait_send()
+
+
+def finish(raw_ref, mean_ref, out_ref, rms_ref):
+    mean_square = mean_ref[0:1, 0:1]
+    out_ref[...] = raw_ref[...] * lax.rsqrt(mean_square + norm_eps)
+    rms_ref[...] = jnp.sqrt(mean_square)
 
 
 def solution(mesh):
@@ -758,6 +788,10 @@
             pltpu.VMEM((32, 256), BF16),
             pltpu.VMEM((384, 128), BF16),
             pltpu.VMEM((256, 384), BF16),
+            pltpu.VMEM((128, 384), BF16),
+            pltpu.VMEM((384, 256), BF16),
+            pltpu.VMEM((384, 128), F32),
+            pltpu.VMEM((256, 384), F32),
             pltpu.VMEM((256, 128), F32),
             pltpu.VMEM((256, 128), F32),
             pltpu.SemaphoreType.DMA((5,)),
@@ -768,13 +802,13 @@
             functools.partial(kernel, sizes),
             out_shape=(
                 jax.ShapeDtypeStruct((64, 128), F32),
-                jax.ShapeDtypeStruct((64, 128), F32),
+                jax.ShapeDtypeStruct((8, 128), F32),
             ),
             in_specs=[anywhere] * 4,
             out_specs=(inside, inside),
             scratch_shapes=scratch,
             compiler_params=pltpu.CompilerParams(
-                collective_id=0, has_side_effects=True, vmem_limit_bytes=56470528
+                collective_id=0, has_side_effects=True, vmem_limit_bytes=56491008
             ),
         )(
             populations.reshape(19, 64, 128),
@@ -782,7 +816,18 @@
             flags.reshape(64, 128),
             adjoint_seed.reshape(19, 64, 128),
         )
-        return grad.reshape(8, 8, 128) * lax.rsqrt(rms.reshape(8, 8, 128) * rms.reshape(8, 8, 128) + norm_eps), jnp.max(rms.reshape(8, 8, 128))
+        grad, rms = pl.pallas_call(
+            finish,
+            out_shape=(
+                jax.ShapeDtypeStruct((64, 128), F32),
+                jax.ShapeDtypeStruct((1, 1), F32),
+            ),
+            in_specs=[inside, inside],
+            out_specs=(inside, inside),
+            name="scale_gradient",
+            compiler_params=pltpu.CompilerParams(vmem_limit_bytes=1024 * 1024),
+        )(grad, rms)
+        return grad.reshape(8, 8, 128), rms.reshape(())
 
     return jax.shard_map(
         body,

time: 39.4 us -> 38.8 us (0.985)
  other arithmetic: 1.23 us -> 0 us
  Pallas kernels: 37.4 us -> 38.1 us
    reduce_max x1 -> x0, other arithmetic: 1.23 us -> none  [body(): jnp.max(rms.reshape(8, 8, 128))]
    pallas_call x0 -> x1, Pallas kernels: none -> 0.66 us  [body(): pl.pallas_call(finish, out_shape=(jax.ShapeDtypeStruct((64, 128), F32), j...]
where the time goes in v4:
time: 38.8 us; the launch traced here: 38.7 us
  Pallas kernels  38.1 us (98%)
  between operations  0.64 us (2%)
    pallas_call x1, Pallas kernels, body(): pl.pallas_call(functools.partial(kernel, sizes), out_shape=(jax.ShapeDtyp...  37.4 us

profile of v4, /device:TPU:1, one launch (start us, length us, event | category | flops | bytes accessed | tf_op | source)
XLA Modules:
  0.0 38.7 jit_solution(8160108803863586024)
XLA Ops:
  0.6 37.4 %shard_map.59 = (f32[64,128]{1,0:T(8,128)S(1)}, f32[8,128]{1,0:T(8,128)S(1)}) custom-call(f32[19,64,128]{2,1,0:T(8,128)} %bitcast.6, f32[64,128]{1,0:T(8,128)} %bitcast.8, s32[64,128]{1,0:T(8,128)} %bitcast.9, f32[19,64,128]{2,1,0:T(8,128)} %bitcast.7), custom_call_target="tpu_custom_call" | custom-call | tf_op jit(solution)/shard_map/pallas_call | solution.py:801
  38.0 0.7 %scale_gradient.1 = (f32[64,128]{1,0:T(8,128)}, f32[1,1]{1,0:T(1,128)}) custom-call(f32[64,128]{1,0:T(8,128)S(1)} %get-tuple-element.6.raw_ref, f32[8,128]{1,0:T(8,128)S(1)} %get-tuple-element.7.mean_ref), custom_call_target="tpu_custom_call" | custom-call | tf_op jit(solution)/shard_map/scale_gradient/pallas_call | solution.py:819

commit v5 on v4

--- a/solution.py
+++ b/solution.py
@@ -467,13 +467,6 @@
             field_copies.append(send(source, target, flow))
     for b in (1, -1):
         field_copies.append(send(y_field.at[side[b]], field.at[region(0, -b)], (0, b, 0)))
-    for a in (1, -1):
-        fill_copies.append(send(x_send.at[side[a]], x_recv.at[side[a]], (a, 0, 0)))
-    for b in (1, -1):
-        fill_copies.append(
-            send(y_send.at[side[b]], y_rows.at[side[b], :, pl.ds(8, 8), :], (0, b, 0))
-        )
-
     def one_if(condition):
         return jnp.where(condition, 1.0, 0.0).astype(F32)
 
@@ -520,6 +513,13 @@
         return carry
 
     lax.fori_loop(0, 16, build_rows, 0)
+    for a in (1, -1):
+        fill_copies.append(send(x_send.at[side[a]], x_recv.at[side[a]], (a, 0, 0)))
+    for b in (1, -1):
+        fill_copies.append(
+            send(y_send.at[side[b]], y_rows.at[side[b], :, pl.ds(8, 8), :], (0, b, 0))
+        )
+
     big_lt[...] = big_l_wide[...].T.astype(BF16)
     rep_lt[...] = rep_l_wide[...].T[0:32, :].astype(BF16)
 
@@ -571,7 +571,8 @@
     halo_xy = left_dot(rep_l[...], halo_x) * block_mask[...]
     summed = right_dot(jnp.concatenate([inner_xy, halo_xy], axis=1), cross_z[...])
     scale_rows = jnp.concatenate([row_scale[...]] * 3, axis=1)
-    kappa_v[...] = 0.5 * (1.0 - summed * scale_rows * lane_scale)
+    scale_all = scale_rows * (-0.5 * lane_scale)
+    kappa_v[...] = 0.5 + summed * scale_all
 
     for copy in fill_copies[2:]:
         copy.wait_recv()
@@ -669,9 +670,9 @@
             ]
     lax.fori_loop(0, 2, lambda n, carry: plane_step(7 * n, carry), 0, unroll=2)
 
-    scaled = grad_v[...] * (scale_rows * (-0.5 * lane_scale))
+    scaled = grad_v[...] * scale_all
     summed = right_dot(scaled, cross_zt[...])
-    spread[...] = left_dot(big_lt[...], summed[:, 0:128])
+    spread[pl.ds(64, 320), :] = left_dot(big_lt[pl.ds(64, 320), :], summed[:, 0:128])
     spread_copies = []
     for flow in flows:
         a, b, c = flow
@@ -690,6 +691,7 @@
             spread_copies.append(
                 send(q_out.at[3 * (b + 1) + a + 1], q_recv.at[flow_index[flow]], flow)
             )
+    spread[pl.ds(0, 64), :] = left_dot(big_lt[pl.ds(0, 64), :], summed[:, 0:128])
     arrived = dict(zip([f for f in flows if f[2] == 0] + [f for f in flows if f[2] != 0], spread_copies))
     for b in (1, -1):
         arrived[0, b, 0].wait_recv()
@@ -725,21 +727,30 @@
         tile = spread[pl.ds(8 * x, 8), :]
         squares = squares + tile * tile
 
+    result_copy = pltpu.make_async_copy(spread.at[pl.ds(0, 64)], out_ref, local_sem.at[0])
+    result_copy.start()
+
     mine = gy * nz + gz
     ring_a[mine] = jnp.sum(squares, axis=0, keepdims=True)
+    before = list(started)
     ring_copies = [send(ring_a.at[mine], ring_a.at[mine], move) for move in slab_moves]
+    for copy in before:
+        copy.wait_send()
     for copy in reversed(ring_copies):
         copy.wait_recv()
     ring_b[gx] = jnp.sum(ring_a[...], axis=0)
+    before = ring_copies
     ring_copies = [send(ring_b.at[gx], ring_b.at[gx], move) for move in line_moves]
+    for copy in before:
+        copy.wait_send()
+    result_copy.wait()
+    for copy in ring_copies:
+        copy.wait_send()
     for copy in reversed(ring_copies):
         copy.wait_recv()
     total = jnp.sum(jnp.sum(ring_b[...], axis=0), axis=1, keepdims=True)
     mean_square = total / (8192.0 * nx * ny * nz)
-    out_ref[...] = spread[pl.ds(0, 64), :]
     rms_ref[...] = jnp.broadcast_to(mean_square, (8, 128))
-    for copy in started:
-        copy.wait_send()
 
 
 def finish(raw_ref, mean_ref, out_ref, rms_ref):
@@ -805,7 +816,7 @@
                 jax.ShapeDtypeStruct((8, 128), F32),
             ),
             in_specs=[anywhere] * 4,
-            out_specs=(inside, inside),
+            out_specs=(anywhere, inside),
             scratch_shapes=scratch,
             compiler_params=pltpu.CompilerParams(
                 collective_id=0, has_side_effects=True, vmem_limit_bytes=56491008

time: 38.8 us -> 38.7 us (level)
  no operation moved by 1% of the time
where the time goes in v5:
time: 38.7 us; the launch traced here: 38.6 us
  Pallas kernels  38 us (98%)
  between operations  0.64 us (2%)
    pallas_call x1, Pallas kernels, body(): pl.pallas_call(functools.partial(kernel, sizes), out_shape=(jax.ShapeDtyp...  37.3 us

profile of v5, /device:TPU:1, one launch (start us, length us, event | category | flops | bytes accessed | tf_op | source)
XLA Modules:
  0.0 38.6 jit_solution(14684408525435330013)
XLA Ops:
  0.6 37.3 %shard_map.59 = (f32[64,128]{1,0:T(8,128)S(1)}, f32[8,128]{1,0:T(8,128)S(1)}) custom-call(f32[19,64,128]{2,1,0:T(8,128)} %bitcast.6, f32[64,128]{1,0:T(8,128)} %bitcast.8, s32[64,128]{1,0:T(8,128)} %bitcast.9, f32[19,64,128]{2,1,0:T(8,128)} %bitcast.7), custom_call_target="tpu_custom_call" | custom-call | tf_op jit(solution)/shard_map/pallas_call | solution.py:812
  38.0 0.7 %scale_gradient.1 = (f32[64,128]{1,0:T(8,128)}, f32[1,1]{1,0:T(1,128)}) custom-call(f32[64,128]{1,0:T(8,128)S(1)} %get-tuple-element.6.raw_ref, f32[8,128]{1,0:T(8,128)S(1)} %get-tuple-element.7.mean_ref), custom_call_target="tpu_custom_call" | custom-call | tf_op jit(solution)/shard_map/scale_gradient/pallas_call | solution.py:830

commit v6 on v4

--- a/solution.py
+++ b/solution.py
@@ -258,6 +258,7 @@
     first_v,
     slope_v,
     seed_v,
+    turned,
     field,
     x_send,
     x_recv,
@@ -520,6 +521,23 @@
         return carry
 
     lax.fori_loop(0, 16, build_rows, 0)
+
+    def turn(tile, j):
+        _, b, c = velocities[j]
+        if b != 0:
+            tile = pltpu.roll(tile, b % 8, 0)
+        if c != 0:
+            tile = pltpu.roll(tile, c % 128, 1)
+        return tile
+
+    def turn_step(x, carry):
+        inner = pl.ds(aligned(x + 1), 8)
+        for k in range(3):
+            for j in range(1, 19):
+                turned[k, j - 1, inner, :] = turn(own(k, j, inner), j)
+        return carry
+
+    lax.fori_loop(0, 8, turn_step, 0, unroll=2)
     big_lt[...] = big_l_wide[...].T.astype(BF16)
     rep_lt[...] = rep_l_wide[...].T[0:32, :].astype(BF16)
 
@@ -575,6 +593,13 @@
 
     for copy in fill_copies[2:]:
         copy.wait_recv()
+    for b in (1, -1):
+        for s, j in enumerate(crossing[1, b]):
+            c = velocities[j][2]
+            for k in range(3):
+                if c != 0:
+                    lines = y_rows[side[b], 5 * k + s, pl.ds(8, 8), :]
+                    y_rows[side[b], 5 * k + s, pl.ds(8, 8), :] = pltpu.roll(lines, c % 128, 1)
     eighth = lax.shift_right_logical(lane, 3)
     slot = eighth - jnp.where(eighth >= 10, 10, jnp.where(eighth >= 5, 5, 0))
     for sign in (1, -1):
@@ -602,13 +627,11 @@
     def plane_step(x, carry):
         def stream(k, j):
             a, b, c = velocities[j]
-            tile = own(k, j, pl.ds(aligned(x + 1 - a), 8))
+            tile = turned[k, j - 1, pl.ds(aligned(x + 1 - a), 8), :]
             if b != 0:
                 s = crossing[1, b].index(j)
                 line = y_rows[side[b], 5 * k + s, pl.ds(8 + x - a, 1), :]
-                tile = jnp.where(
-                    row == (0 if b == 1 else 7), line, pltpu.roll(tile, b % 8, 0)
-                )
+                tile = jnp.where(row == (0 if b == 1 else 7), line, tile)
             if c != 0:
                 s = crossing[2, c].index(j)
                 edge = 0 if c == 1 else 127
@@ -616,7 +639,7 @@
                 column = pltpu.roll(
                     z_pack[side[c]], jnp.bitwise_and(256 + edge - place, 127), 1
                 )
-                tile = jnp.where(lane == edge, column, pltpu.roll(tile, c % 128, 1))
+                tile = jnp.where(lane == edge, column, tile)
             return tile
 
         def spot(j):
@@ -656,9 +679,8 @@
         n = side[sign]
         rows = pl.ds(0, 8) if sign == 1 else pl.ds(72, 8)
         for s, j in enumerate(crossing[0, sign]):
-            first_v[j, rows, :] = x_recv[n, s]
-            slope_v[(j - 1) // 2, rows, :] = x_recv[n, 5 + s]
-            seed_v[opposite[j], rows, :] = x_recv[n, 10 + s]
+            for k in range(3):
+                turned[k, j - 1, rows, :] = turn(x_recv[n, 5 * k + s], j)
     for a, b in diagonals:
         j = velocities.index((a, b, 0))
         s = crossing[1, b].index(j)
@@ -761,6 +783,7 @@
             pltpu.VMEM((19, 80, 128), F32),
             pltpu.VMEM((9, 80, 128), F32),
             pltpu.VMEM((19, 80, 128), F32),
+            pltpu.VMEM((3, 18, 80, 128), F32),
             pltpu.VMEM((384, 128), F32),
             pltpu.VMEM((2, 15, 8, 128), F32),
             pltpu.VMEM((2, 15, 8, 128), F32),

time: 38.8 us -> 38.7 us (level)
  no operation moved by 1% of the time
where the time goes in v6:
time: 38.7 us; the launch traced here: 38.6 us
  Pallas kernels  38 us (98%)
  between operations  0.64 us (2%)
    pallas_call x1, Pallas kernels, body(): pl.pallas_call(functools.partial(kernel, sizes), out_shape=(jax.ShapeDtyp...  37.3 us

profile of v6, /device:TPU:1, one launch (start us, length us, event | category | flops | bytes accessed | tf_op | source)
XLA Modules:
  0.0 38.6 jit_solution(8080626151166379173)
XLA Ops:
  0.6 37.3 %shard_map.59 = (f32[64,128]{1,0:T(8,128)S(1)}, f32[8,128]{1,0:T(8,128)S(1)}) custom-call(f32[19,64,128]{2,1,0:T(8,128)} %bitcast.6, f32[64,128]{1,0:T(8,128)} %bitcast.8, s32[64,128]{1,0:T(8,128)} %bitcast.9, f32[19,64,128]{2,1,0:T(8,128)} %bitcast.7), custom_call_target="tpu_custom_call" | custom-call | tf_op jit(solution)/shard_map/pallas_call | solution.py:824
  37.9 0.7 %scale_gradient.1 = (f32[64,128]{1,0:T(8,128)}, f32[1,1]{1,0:T(1,128)}) custom-call(f32[64,128]{1,0:T(8,128)S(1)} %get-tuple-element.6.raw_ref, f32[8,128]{1,0:T(8,128)S(1)} %get-tuple-element.7.mean_ref), custom_call_target="tpu_custom_call" | custom-call | tf_op jit(solution)/shard_map/scale_gradient/pallas_call | solution.py:842
